TPU v7x, 128 devices: a whole 4x4x4 slice. The times are simulated.
128 devices in a mesh: row: 8 (over z, core), col: 16 (over x, y).
Axes of the slice: x: 4, y: 4, z: 4, core: 2. Of those that a mesh axis runs over, the one named last changes fastest.
Arguments:
- cotangent: bfloat16 [524288, 128], P(('row', 'col')), may hold values from -0.0625 to 0.0625
- owner_row: int32 [524288], P(('row', 'col')), may hold values from 0 to 7, as said below
- owner_slot: int32 [524288], P(('row', 'col')), may hold values from 0 to 1535, as said below
- counts: int32 [128], P(('row', 'col')), may hold values from 1 to 1536, as said below
- unique_ids: int32 [196608], P(('row', 'col')), may hold values from 0 to 4194303
- hash_seeds: int32 [3, 1024], replicated, may hold values from 1 to 32767
- w_in: bfloat16 [1024, 1024], replicated, may hold values from -0.1875 to 0.1875
- w_mid: bfloat16 [1024, 1024], replicated, may hold values from -0.1875 to 0.1875
- w_out: bfloat16 [1024, 128], replicated, may hold values from -0.1875 to 0.1875
Outputs:
- grad_in: float32 [1024, 1024], P(('row', 'col'))
- grad_mid: float32 [1024, 1024], P(('row', 'col'))
- grad_out: float32 [1024, 128], P(('row', 'col'))
Inputs may be any that keep to these rules, and one draw needn't show every extreme that they name: `owner_row`: A device sends at most 1536 lookups to one owner and exactly 1536 to one owner of its column; all devices of a column send equally many lookups to a given owner. `owner_slot`: A lookup's slot is below the count of its owner (the device at row owner_row in the lookup's column). The counts of the 8 devices of one column sum to 4096, and one device of each column has 1536.
All inputs are finite; a program needn't handle non-finite values.
Results may differ from a plain program's by a relative error of at most 0.0058.
Values may be sent and summed in bfloat16 or wider, within the bound.
No kernel may reach another device: no remote copies, remote signals or barrier semaphores. Data moves between devices by JAX's collectives and lax.ppermute only.
A program may use at most 128 MiB of HBM per device.

v0:
```python
import jax
import jax.numpy as jnp
from jax import lax
from jax.experimental import pallas as pl
from jax.experimental.pallas import tpu as pltpu
from jax.sharding import Mesh, PartitionSpec as P

PRIME = 65521
HIGH_PRIME = 32749
SLOTS = 1536
LOOKUPS = 4096
WIDTH = 1024
EMBED = 128
SHARE = 512
ALL = ("z", "core", "x", "y")
VMEM_LIMIT = 24 * 1024 * 1024
PACK_LIMIT = 24 * 1024 * 1024
BY_COLUMN = tuple(z * 16 + column for column in range(16) for z in range(4))
BF16 = jnp.bfloat16
F32 = jnp.float32
I32 = jnp.int32


def vmem(count):
    return [pl.BlockSpec(memory_space=pltpu.VMEM)] * count


def params(limit=VMEM_LIMIT):
    return pltpu.CompilerParams(vmem_limit_bytes=limit)


def owner_ranges(table_ref):
    first = jnp.zeros((1, 1), I32)
    ranges = []
    for owner in range(8):
        count = table_ref[owner * 16 + 12 : owner * 16 + 13, 0:1]
        ranges.append((first, count))
        first = first + count
    return ranges


def segment_kernel(table_ref, row_ref, slot_ref, cot_ref, keep_ref, send_ref, wide, hot):
    z, core = lax.axis_index("z"), lax.axis_index("core")
    owner = row_ref[...]
    place = slot_ref[...]
    for index, (first, _) in enumerate(owner_ranges(table_ref)):
        place = jnp.where(owner == index, place + first, place)
    place = place ^ (core << 9)
    quarter = ((place >> 10) - z) & 3
    inner = place & 1023
    quarter_t = quarter.T
    ids = lax.broadcasted_iota(I32, (1024, 128), 0)
    for chunk in range(32):
        rows = slice(chunk * 128, chunk * 128 + 128)
        column = jnp.broadcast_to(quarter_t[:, chunk : chunk + 1], (128, 128))
        cot = cot_ref[rows, :].astype(F32)
        for part in range(4):
            wide[rows, part * 128 : part * 128 + 128] = jnp.where(column == part, cot, 0.0).astype(BF16)
        hot[:, rows] = jnp.where(inner[chunk : chunk + 1, :] == ids, 1.0, 0.0).astype(BF16)
    for pair in range(2):
        total = jnp.dot(hot[...], wide[:, pair * 256 : pair * 256 + 256], preferred_element_type=F32)
        for sub in range(2):
            part = pair * 2 + sub
            rows = slice(part * 512, part * 512 + 512)
            cols = slice(sub * 128, sub * 128 + 128)
            keep_ref[rows, :] = total[0:512, cols]
            send_ref[rows, :] = total[512:1024, cols].astype(BF16)


def join_kernel(keep_ref, got_ref, after_ref, own_ref, one_ref, two_ref, three_ref):
    own_ref[...] = keep_ref[0:512, :] + got_ref[0:512, :].astype(F32)
    for part, out in enumerate((one_ref, two_ref, three_ref), 1):
        rows = slice(part * 512, part * 512 + 512)
        out[...] = (keep_ref[rows, :] + got_ref[rows, :].astype(F32)).astype(BF16)


def total_kernel(own_ref, one_ref, two_ref, three_ref, after_ref, out_ref):
    total = own_ref[...] + one_ref[...].astype(F32) + two_ref[...].astype(F32) + three_ref[...].astype(F32)
    out_ref[...] = total.astype(BF16)


def mish_parts(value):
    e = jnp.exp(jnp.minimum(value, 20.0))
    n = e * (e + 2.0)
    inverse = 1.0 / (n + 2.0)
    tanh_soft = n * inverse
    twice = inverse + inverse
    return value * tanh_soft, tanh_soft + (value * (n - e)) * (twice * twice)


def pack_kernel(count_ref, ids_ref, cot_ref, row_ref, slot_ref,
                out_ref, cot_out, row_out, slot_out, ids, sems):
    pairs = ((ids_ref, ids), (cot_ref, cot_out), (row_ref, row_out), (slot_ref, slot_out))
    copies = [pltpu.make_async_copy(source, target, sems.at[index]) for index, (source, target) in enumerate(pairs)]
    for copy in copies:
        copy.start()
    copies[0].wait()
    for copy in range(8):
        out_ref[copy, 0:12, :] = ids[...]
        out_ref[copy, 12:16, :] = jnp.full((4, 128), count_ref[0], I32)
    for copy in copies[1:]:
        copy.wait()


def prepare_kernel(w_in_ref, w_mid_ref, w_out_ref, seeds_ref, after_ref,
                   w_in_t_ref, w_mid_t_ref, w_out_on_chip_ref, seeds_t_ref):
    for part in range(4):
        cols = slice(part * 256, part * 256 + 256)
        w_in_t_ref[cols, :] = w_in_ref[:, cols].T
        w_mid_t_ref[cols, :] = w_mid_ref[:, cols].T
    w_out_on_chip_ref[...] = w_out_ref[...]
    seeds_t_ref[...] = jnp.concatenate([seeds_ref[...], jnp.zeros((5, WIDTH), I32)], axis=0).T


def find_ids(z, core, table_ref):
    line = lax.broadcasted_iota(I32, (1, WIDTH), 1)
    place = z * 1024 + (line ^ (core << 9))
    where_at = jnp.zeros((1, WIDTH), I32)
    for index, (first, count) in enumerate(owner_ranges(table_ref)):
        inside = (place >= first) & (place < first + count)
        where_at = jnp.where(inside, place - first + index * 2048, where_at)
    sub = lax.broadcasted_iota(I32, (128, WIDTH), 0)
    pick = jnp.where((where_at >> 7) == sub, 1.0, 0.0).astype(BF16)
    table = table_ref[...].T
    found = jnp.zeros((128, WIDTH), F32)
    for shift_by in (0, 8, 16):
        piece = ((table >> shift_by) & 255).astype(F32).astype(BF16)
        found += jnp.dot(piece, pick, preferred_element_type=F32) * float(1 << shift_by)
    return jnp.sum(jnp.where((where_at & 127) == sub, found, 0.0), axis=0, keepdims=True).astype(I32)


def forward_kernel(table_ref, after_ref, seeds_ref, w_in_ref, w_mid_ref,
                   slope_one_ref, slope_two_ref, own_ref, send_ref, other_ref, codes, enc, one, two):
    z, core = lax.axis_index("z"), lax.axis_index("core")
    ids = find_ids(z, core, table_ref)
    low = (ids >> 16) * 15 + (ids & 65535)
    over = low >= PRIME
    high = (ids >> 16) + jnp.where(over, 1, 0)
    codes[0:1, :] = jnp.where(over, low - PRIME, low)
    codes[1:2, :] = jnp.where(high >= HIGH_PRIME, high - HIGH_PRIME, high)
    def encode(rows, cols):
        first, second, offset = (seeds_ref[rows, index : index + 1] for index in range(3))
        mix = first * codes[0:1, cols] + (second * codes[1:2, cols] + offset)
        mix = lax.shift_right_logical(mix, 16) * 15 + (mix & 65535)
        mix = (mix >> 16) * 15 + (mix & 65535)
        mix = jnp.where(mix >= PRIME, mix - PRIME, mix)
        return (mix.astype(F32) * (2.0 / 65520.0) - 1.0).astype(BF16)

    for block in range(2):
        cols = slice(block * 256, block * 256 + 256)
        for part in range(4):
            rows = slice(part * 256, part * 256 + 256)
            enc[rows, cols] = encode(rows, cols)
        for weights, source, target, slopes in (
            (w_in_ref, enc, one, slope_one_ref), (w_mid_ref, one, two, slope_two_ref)):
            for part in range(4):
                rows = slice(part * 256, part * 256 + 256)
                act, slope = mish_parts(jnp.dot(weights[rows, :], source[:, cols], preferred_element_type=F32))
                target[rows, cols] = act.astype(BF16)
                slopes[rows, cols] = slope
    for part in range(4):
        mine = pl.ds(pl.multiple_of(core * 128 + part * 256, 128), 128)
        theirs = pl.ds(pl.multiple_of((core ^ 1) * 128 + part * 256, 128), 128)
        for layer, source in enumerate((enc, one, two)):
            start = layer * 512 + part * 128
            own_ref[start : start + 128, :] = source[mine, :]
            if layer:
                send_ref[start - 512 : start - 384, :] = source[theirs, :]
        other_ref[part * 128 : part * 128 + 128, :] = encode(mine, slice(512, 1024))


NT = (((1,), (1,)), ((), ()))
TILES = tuple(slice(index * 256, index * 256 + 256) for index in range(4))


def delta_two_kernel(grad_ref, slope_ref, w_out_ref, delta_ref):
    for rows in TILES:
        back = lax.dot_general(w_out_ref[rows, :], grad_ref[...], NT, preferred_element_type=F32)
        delta_ref[rows, :] = (back * slope_ref[rows, :]).astype(BF16)
    delta_ref[1024:1152, :] = grad_ref[...].astype(F32).T.astype(BF16)


def delta_one_kernel(delta_two_ref, slope_ref, w_mid_ref, delta_ref):
    for rows in TILES:
        back = jnp.dot(w_mid_ref[rows, :], delta_two_ref[0:1024, :], preferred_element_type=F32)
        delta_ref[rows, :] = (back * slope_ref[rows, :]).astype(BF16)


def over_slots(own, delta, got, got_delta):
    return (lax.dot_general(own, delta, NT, preferred_element_type=F32)
            + lax.dot_general(got, got_delta, NT, preferred_element_type=F32))


def weights_two_kernel(own_ref, delta_ref, got_ref, got_delta_ref, keep_ref, one_ref, two_ref, three_ref, total):
    for cols in TILES:
        total[:, cols] = over_slots(
            own_ref[512:1024, :], delta_ref[cols, :], got_ref[0:512, :], got_delta_ref[cols, :])
    total[:, 1024:1152] = over_slots(
        own_ref[1024:1536, :], delta_ref[1024:1152, :], got_ref[512:1024, :], got_delta_ref[1024:1152, :])
    z = lax.axis_index("z")
    for step, out_ref in enumerate((keep_ref, one_ref, two_ref, three_ref)):
        rows = pl.ds(pl.multiple_of(((z + step) & 3) * 128, 128), 128)
        out_ref[...] = total[rows, :].astype(out_ref.dtype)


def weights_one_kernel(own_ref, delta_ref, other_ref, got_delta_ref, after_ref, out_ref):
    for cols in TILES:
        value = over_slots(own_ref[0:512, :], delta_ref[cols, :], other_ref[...], got_delta_ref[cols, :])
        out_ref[:, cols] = jnp.concatenate(
            [value[chip * 8 : chip * 8 + 8, :] for chip in BY_COLUMN], axis=0).astype(BF16)


def sum_columns_kernel(pieces_ref, keep_ref, one_ref, two_ref, three_ref, total):
    z = lax.axis_index("z")
    for col in range(0, 1024, 128):
        cols = slice(col, col + 128)
        total[:, cols] = sum(pieces_ref[piece * 32 : piece * 32 + 32, cols].astype(F32) for piece in range(16))
    for step, out_ref in enumerate((keep_ref, one_ref, two_ref, three_ref)):
        out_ref[...] = total[pl.ds(pl.multiple_of(((z + step) & 3) * 8, 8), 8), :]


def sum_rows_kernel(keep_ref, one_ref, two_ref, three_ref, after_ref, out_ref):
    total = keep_ref[...] + one_ref[...].astype(F32) + two_ref[...].astype(F32) + three_ref[...].astype(F32)
    out_ref[...] = total.astype(BF16)


def last_kernel(keep_ref, one_ref, two_ref, three_ref, pieces_ref, in_ref, mid_ref, last_ref):
    in_ref[...] = (keep_ref[...] + one_ref[...]) + (two_ref[...] + three_ref[...])
    for start, out_ref in ((0, mid_ref), (1024, last_ref)):
        for col in range(0, out_ref.shape[1], 128):
            cols = slice(start + col, start + col + 128)
            total = sum(pieces_ref[piece * 16 : piece * 16 + 16, cols].astype(F32) for piece in range(8))
            out_ref[:, col : col + 128] = total[0:8, :] + total[8:16, :]


def shift(steps):
    return [(index, (index + steps) % 4) for index in range(4)]


SWAP = [(0, 1), (1, 0)]


def per_device(cotangent, owner_row, owner_slot, counts, unique_ids, hash_seeds, w_in, w_mid, w_out):
    shape = jax.ShapeDtypeStruct

    anywhere = pl.BlockSpec(memory_space=pl.ANY)
    with jax.named_scope("gather_ids"):
        copies, cot, rows, slots = pl.pallas_call(
            pack_kernel,
            out_shape=(shape((8, 16, 128), I32), shape((LOOKUPS, EMBED), BF16),
                       shape((32, 128), I32), shape((32, 128), I32)),
            in_specs=[pl.BlockSpec(memory_space=pltpu.SMEM)] + [pl.BlockSpec(memory_space=pltpu.HBM)] * 4,
            out_specs=tuple(vmem(4)),
            scratch_shapes=[pltpu.VMEM((12, 128), I32), pltpu.SemaphoreType.DMA((4,))],
            compiler_params=params(PACK_LIMIT),
            name="pack_ids",
        )(counts, *(pltpu.with_memory_space_constraint(value, pltpu.HBM) for value in (
            unique_ids.reshape(12, 128), cotangent, owner_row.reshape(32, 128), owner_slot.reshape(32, 128))))
        table = lax.all_to_all(copies, ("z", "core"), split_axis=0, concat_axis=0, tiled=True).reshape(128, 128)

    keep, send = pl.pallas_call(
        segment_kernel,
        out_shape=(shape((2048, EMBED), F32), shape((2048, EMBED), BF16)),
        in_specs=vmem(4),
        out_specs=tuple(vmem(2)),
        scratch_shapes=[pltpu.VMEM((LOOKUPS, 512), BF16), pltpu.VMEM((1024, LOOKUPS), BF16)],
        compiler_params=params(),
        cost_estimate=pl.CostEstimate(flops=2 * 1024 * 4096 * 512, bytes_accessed=1 << 22, transcendentals=0),
        name="segment_sums",
    )(table, rows, slots, cot)

    with jax.named_scope("exchange_grads"):
        got = lax.ppermute(send, "core", SWAP)
        w_in_t, w_mid_t, w_out, seeds_t = pl.pallas_call(
            prepare_kernel,
            out_shape=(shape((WIDTH, WIDTH), BF16), shape((WIDTH, WIDTH), BF16),
                       shape((WIDTH, EMBED), BF16), shape((WIDTH, 8), I32)),
            in_specs=vmem(4) + [anywhere],
            out_specs=tuple(vmem(4)),
            compiler_params=params(),
            name="transpose_weights",
        )(w_in, w_mid, w_out, hash_seeds, send)
        own, one, two, three = pl.pallas_call(
            join_kernel,
            out_shape=(shape((512, EMBED), F32),) + (shape((512, EMBED), BF16),) * 3,
            in_specs=vmem(2) + [anywhere],
            out_specs=tuple(vmem(4)),
            compiler_params=params(),
            name="join_cores",
        )(keep, got, seeds_t)
        parts = [lax.ppermute(part, "z", shift(step)) for step, part in ((2, two), (1, one), (3, three))]

    slope_one, slope_two, own_units, send_units, other_enc = pl.pallas_call(
        forward_kernel,
        out_shape=(shape((WIDTH, SHARE), F32),) * 2 + (
            shape((3 * 512, SHARE), BF16), shape((2 * 512, SHARE), BF16), shape((512, SHARE), BF16)),
        in_specs=vmem(1) + [anywhere] + vmem(3),
        out_specs=tuple(vmem(5)),
        scratch_shapes=[pltpu.VMEM((8, WIDTH), I32)] + [pltpu.VMEM((WIDTH, SHARE), BF16)] * 3,
        compiler_params=params(),
        cost_estimate=pl.CostEstimate(flops=4 * 1024 ** 3, bytes_accessed=1 << 24, transcendentals=1 << 21),
        name="forward",
    )(table, one, seeds_t, w_in_t, w_mid_t)
    got_units = lax.ppermute(send_units, "core", SWAP)

    with jax.named_scope("grad_use"):
        grads = pl.pallas_call(
            total_kernel,
            out_shape=shape((SHARE, EMBED), BF16),
            in_specs=vmem(4) + [anywhere],
            out_specs=vmem(1)[0],
            compiler_params=params(),
            name="total_grads",
        )(own, *parts, own_units)

    with jax.named_scope("backward"):
        delta_two = pl.pallas_call(
            delta_two_kernel,
            out_shape=shape((1152, SHARE), BF16),
            in_specs=vmem(3),
            out_specs=vmem(1)[0],
            compiler_params=params(),
            name="delta_two",
        )(grads, slope_two, w_out)
        got_delta_two = lax.ppermute(delta_two, "core", SWAP)
        delta_one = pl.pallas_call(
            delta_one_kernel,
            out_shape=shape((WIDTH, SHARE), BF16),
            in_specs=vmem(3),
            out_specs=vmem(1)[0],
            compiler_params=params(),
            cost_estimate=pl.CostEstimate(flops=20 * 1024 ** 3, bytes_accessed=1 << 25, transcendentals=0),
            name="delta_one",
        )(delta_two, slope_one, w_mid)
        got_delta_one = lax.ppermute(delta_one, "core", SWAP)

    with jax.named_scope("sum_devices"):
        keep_two, *pieces = pl.pallas_call(
            weights_two_kernel,
            out_shape=(shape((128, 1152), F32),) + (shape((128, 1152), BF16),) * 3,
            in_specs=vmem(4),
            out_specs=tuple(vmem(4)),
            scratch_shapes=[pltpu.VMEM((512, 1152), F32)],
            compiler_params=params(),
            name="weights_two",
        )(own_units, delta_two, got_units, got_delta_two)
        rows_two = [lax.ppermute(pieces[step - 1], "z", shift(step)) for step in (2, 1, 3)]
        out_one = pl.pallas_call(
            weights_one_kernel,
            out_shape=shape((512, 1024), BF16),
            in_specs=vmem(4) + [anywhere],
            out_specs=vmem(1)[0],
            compiler_params=params(),
            name="weights_one",
        )(own_units, delta_one, other_enc, got_delta_one, pieces[0])
        columns_one = lax.all_to_all(out_one, ("x", "y"), split_axis=0, concat_axis=0, tiled=True)
        keep_one, *pieces = pl.pallas_call(
            sum_columns_kernel,
            out_shape=(shape((8, 1024), F32),) * 4,
            in_specs=vmem(1),
            out_specs=tuple(vmem(4)),
            scratch_shapes=[pltpu.VMEM((32, 1024), F32)],
            compiler_params=params(),
            name="sum_columns",
        )(columns_one)
        rows_one = [lax.ppermute(pieces[step - 1], "z", shift(step)) for step in (2, 1, 3)]
        out_two = pl.pallas_call(
            sum_rows_kernel,
            out_shape=shape((128, 1152), BF16),
            in_specs=vmem(4) + [anywhere],
            out_specs=vmem(1)[0],
            compiler_params=params(),
            name="sum_rows",
        )(keep_two, *rows_two, pieces[0])
        columns_two = lax.all_to_all(out_two, ("x", "y"), split_axis=0, concat_axis=0, tiled=True)
        return pl.pallas_call(
            last_kernel,
            out_shape=(shape((8, 1024), F32), shape((8, 1024), F32), shape((8, EMBED), F32)),
            in_specs=vmem(5),
            out_specs=tuple(vmem(3)),
            compiler_params=params(),
            name="last_sums",
        )(keep_one, *rows_one, columns_two)


def solution(mesh):
    fine = Mesh(mesh.devices.reshape(4, 2, 4, 4), ALL)
    split = P(ALL)
    rows = P(ALL, None)
    return jax.shard_map(
        per_device, mesh=fine, in_specs=(rows, split, split, split, split, P(), P(), P(), P()),
        out_specs=(rows, rows, rows), check_vma=False)
```

profile of v0, /device:TPU:0, one launch (start us, length us, event | category | flops | bytes accessed | tf_op | source)
XLA Modules:
  0.0 80.7 jit_solution(18141169844245453154)
XLA Ops:
  1.3 1.3 %pack_ids.1 = (s32[8,16,128]{2,1,0:T(8,128)S(1)}, bf16[4096,128]{1,0:T(8,128)(2,1)S(1)}, s32[32,128]{1,0:T(8,128)S(1)}, s32[32,128]{1,0:T(8,128)S(1)}) custom-call(s32[1]{0:T(128)S(6)} %copy.12.count_ref, s32[12,128]{1,0:T(8,128)} %bitcast.14, bf16[4096,128]{1,0:T(8,128)(2,1)} %cot_ref.1, s32[32,128]{1,0:T(8,128)} %bitcast.12, s32[32,128]{1,0:T(8,128)} %bitcast.13), custom_call_target="tpu_custom_call" | custom-call | tf_op jit(solution)/shard_map/gather_ids/pack_ids/pallas_call | solution.py:248
  2.6 10.8 %all_to_all.27 = s32[8,16,128]{2,1,0:T(8,128)S(1)} all-to-all(s32[8,16,128]{2,1,0:T(8,128)S(1)} %get-tuple-element.30), channel_id=1, replica_groups=mesh['z'=4,'core'=2,'x'=4,'y'=4] {'z','core'}, dimensions={0} | all-to-all | bytes 131072 | tf_op jit(solution)/shard_map/gather_ids/all_to_all | solution.py:259
  13.4 0.0 copy-start
  13.4 0.0 copy-start.1
  13.4 0.0 copy-start.2
  13.4 0.0 copy-start.3
  13.4 5.8 %segment_sums.1 = (f32[2048,128]{1,0:T(8,128)S(1)}, bf16[2048,128]{1,0:T(8,128)(2,1)S(1)}) custom-call(s32[128,128]{1,0:T(8,128)S(1)} %bitcast.10, s32[32,128]{1,0:T(8,128)S(1)} %get-tuple-element.31.row_ref, s32[32,128]{1,0:T(8,128)S(1)} %get-tuple-element.32.slot_ref, bf16[4096,128]{1,0:T(8,128)(2,1)S(1)} %get-tuple-element.33.cot_ref), custom_call_target="tpu_custom_call" | custom-call | flops 4294967296 | bytes 4194304 | tf_op jit(solution)/shard_map/segment_sums/pallas_call | solution.py:261
  19.2 0.1 collective-permute-start
  19.3 0.0 copy-done
  19.3 0.0 copy-done.1
  19.3 0.0 copy-done.2
  19.3 0.0 copy-done.3
  19.3 1.4 %transpose_weights.1 = (bf16[1024,1024]{1,0:T(8,128)(2,1)S(1)}, bf16[1024,1024]{1,0:T(8,128)(2,1)S(1)}, bf16[1024,128]{1,0:T(8,128)(2,1)S(1)}, s32[1024,8]{1,0:T(8,128)S(1)}) custom-call(bf16[1024,1024]{1,0:T(8,128)(2,1)S(1)} %copy-done, bf16[1024,1024]{1,0:T(8,128)(2,1)S(1)} %copy-done.1, bf16[1024,128]{1,0:T(8,128)(2,1)S(1)} %copy-done.2, ...), custom_call_target="tpu_custom_call" | custom-call | tf_op jit(solution)/shard_map/exchange_grads/transpose_weights/pallas_call | solution.py:274
  20.7 0.5 collective-permute-done.got_ref
  21.2 0.1 join_cores.1
  21.3 0.6 collective-permute-start.2
  21.9 2.1 %collective-permute-start.1 = (bf16[512,128]{1,0:T(8,128)(2,1)S(1)}, bf16[512,128]{1,0:T(8,128)(2,1)S(1)}, u32[]{:S(2)}, u32[]{:S(2)}) collective-permute-start(bf16[512,128]{1,0:T(8,128)(2,1)S(1)} %get-tuple-element.42), channel_id=1, source_target_pairs={{0,64},{32,96},{64,0},{96,32},{1,65},{33,97},{65,1},{97,33},{2,66}... | collective-permute-start | bytes 393224 | tf_op jit(solution)/shard_map/exchange_grads/ppermute | solution.py:291
  24.0 1.0 %collective-permute-start.3 = (bf16[512,128]{1,0:T(8,128)(2,1)S(1)}, bf16[512,128]{1,0:T(8,128)(2,1)S(1)}, u32[]{:S(2)}, u32[]{:S(2)}) collective-permute-start(bf16[512,128]{1,0:T(8,128)(2,1)S(1)} %get-tuple-element.43), channel_id=1, source_target_pairs={{0,96},{32,0},{64,32},{96,64},{1,97},{33,1},{65,33},{97,65},{2,98}... | collective-permute-start | bytes 393224 | tf_op jit(solution)/shard_map/exchange_grads/ppermute | solution.py:291
  25.0 6.2 %forward.1 = (f32[1024,512]{1,0:T(8,128)S(1)}, f32[1024,512]{1,0:T(8,128)S(1)}, bf16[1536,512]{1,0:T(8,128)(2,1)S(1)}, bf16[1024,512]{1,0:T(8,128)(2,1)S(1)}, bf16[512,512]{1,0:T(8,128)(2,1)S(1)}) custom-call(s32[128,128]{1,0:T(8,128)S(1)} %bitcast.11, bf16[512,128]{1,0:T(8,128)(2,1)S(1)} %get-tuple-element.37.after_ref, ...), custom_call_target="tpu_custom_call" | custom-call | flops 4294967296 | bytes 16777216 | tf_op jit(solution)/shard_map/forward/pallas_call | solution.py:293
  31.1 0.1 collective-permute-start.5
  31.2 0.0 collective-permute-done.2.two_ref
  31.2 0.0 collective-permute-done.1.one_ref
  31.3 0.3 collective-permute-done.3.three_ref
  31.5 0.1 total_grads.1.grad_ref
  31.6 0.4 delta_two.1.delta_two_ref.delta_ref
  32.0 0.3 collective-permute-start.6
  32.3 1.2 %delta_one.1.delta_ref = bf16[1024,512]{1,0:T(8,128)(2,1)S(1)} custom-call(bf16[1152,512]{1,0:T(8,128)(2,1)S(1)} %delta_two.1.delta_two_ref.delta_ref, f32[1024,512]{1,0:T(8,128)S(1)} %get-tuple-element.46.slope_ref, bf16[1024,1024]{1,0:T(8,128)(2,1)S(1)} %copy-done.1), custom_call_target="tpu_custom_call" | custom-call | flops 21474836480 | bytes 33554432 | tf_op jit(solution)/shard_map/backward/delta_one/pallas_call | solution.py:326
  33.6 0.4 collective-permute-start.4
  33.9 0.0 collective-permute-done.5.got_ref
  33.9 1.6 %collective-permute-done.6.got_delta_ref = bf16[1152,512]{1,0:T(8,128)(2,1)S(1)} collective-permute-done((bf16[1152,512]{1,0:T(8,128)(2,1)S(1)}, bf16[1152,512]{1,0:T(8,128)(2,1)S(1)}, u32[]{:S(2)}, u32[]{:S(2)}) %collective-permute-start.6) | collective-permute-done | bytes 1179680 | tf_op jit(solution)/shard_map/backward/ppermute | solution.py:325
  35.6 1.8 %weights_two.1 = (f32[128,1152]{1,0:T(8,128)S(1)}, bf16[128,1152]{1,0:T(8,128)(2,1)S(1)}, bf16[128,1152]{1,0:T(8,128)(2,1)S(1)}, bf16[128,1152]{1,0:T(8,128)(2,1)S(1)}) custom-call(bf16[1536,512]{1,0:T(8,128)(2,1)S(1)} %get-tuple-element.40.after_ref.own_ref, bf16[1152,512]{1,0:T(8,128)(2,1)S(1)} %delta_two.1.delta_two_ref.delta_ref, ...), custom_call_target="tpu_custom_call" | custom-call | tf_op jit(solution)/shard_map/sum_devices/weights_two/pallas_call | solution.py:338
  37.3 0.0 collective-permute-done.4.got_delta_ref
  37.3 2.3 %weights_one.1 = bf16[512,1024]{1,0:T(8,128)(2,1)} custom-call(bf16[1536,512]{1,0:T(8,128)(2,1)S(1)} %get-tuple-element.40.after_ref.own_ref, bf16[1024,512]{1,0:T(8,128)(2,1)S(1)} %delta_one.1.delta_ref, bf16[512,512]{1,0:T(8,128)(2,1)S(1)} %get-tuple-element.47.other_ref, bf16[1024,512]{1,0:T(8,128)(2,1)S(1)} %collective-permute-done.4.got_delta_ref, ...), custom_call_target="tpu_custom_call" | custom-call | tf_op jit(solution)/shard_map/sum_devices/weights_one/pallas_call | solution.py:348
  39.6 7.0 %all-to-all-start.1 = ((bf16[16,32,1024]{2,1,0:T(8,128)(2,1)}), bf16[16,32,1024]{2,1,0:T(8,128)(2,1)S(1)}, u32[]{:S(2)}, u32[]{:S(2)}) async-start(bf16[16,32,1024]{2,1,0:T(8,128)(2,1)} %bitcast.4), calls=%async_computation.1 | async-start | bytes 2097152 | tf_op jit(solution)/shard_map/sum_devices/all_to_all | solution.py:356
  46.7 1.1 %collective-permute-start.11 = (bf16[128,1152]{1,0:T(8,128)(2,1)S(1)}, bf16[128,1152]{1,0:T(8,128)(2,1)S(1)}, u32[]{:S(2)}, u32[]{:S(2)}) collective-permute-start(bf16[128,1152]{1,0:T(8,128)(2,1)S(1)} %get-tuple-element.49.after_ref), channel_id=1, source_target_pairs={{0,32},{32,64},{64,96},{96,0},{1,33},{33,65},{65,97},{97,1},{2,34}... | collective-permute-start | bytes 884744 | tf_op jit(solution)/shard_map/sum_devices/ppermute | solution.py:347
  47.8 2.2 %collective-permute-start.10 = (bf16[128,1152]{1,0:T(8,128)(2,1)S(1)}, bf16[128,1152]{1,0:T(8,128)(2,1)S(1)}, u32[]{:S(2)}, u32[]{:S(2)}) collective-permute-start(bf16[128,1152]{1,0:T(8,128)(2,1)S(1)} %get-tuple-element.55), channel_id=1, source_target_pairs={{0,64},{32,96},{64,0},{96,32},{1,65},{33,97},{65,1},{97,33},{2,66}... | collective-permute-start | bytes 884744 | tf_op jit(solution)/shard_map/sum_devices/ppermute | solution.py:347
  50.0 1.9 %collective-permute-start.12 = (bf16[128,1152]{1,0:T(8,128)(2,1)S(1)}, bf16[128,1152]{1,0:T(8,128)(2,1)S(1)}, u32[]{:S(2)}, u32[]{:S(2)}) collective-permute-start(bf16[128,1152]{1,0:T(8,128)(2,1)S(1)} %get-tuple-element.56), channel_id=1, source_target_pairs={{0,96},{32,0},{64,32},{96,64},{1,97},{33,1},{65,33},{97,65},{2,98}... | collective-permute-start | bytes 884744 | tf_op jit(solution)/shard_map/sum_devices/ppermute | solution.py:347
  51.9 12.9 %all-to-all-done.1 = bf16[16,32,1024]{2,1,0:T(8,128)(2,1)S(1)} async-done(((bf16[16,32,1024]{2,1,0:T(8,128)(2,1)}), bf16[16,32,1024]{2,1,0:T(8,128)(2,1)S(1)}, u32[]{:S(2)}, u32[]{:S(2)}) %all-to-all-start.1) | async-done | bytes 1048608 | tf_op jit(solution)/shard_map/sum_devices/all_to_all | solution.py:356
  64.8 0.2 sum_columns.1
  65.0 0.0 collective-permute-done.10.one_ref
  65.0 0.0 collective-permute-done.11.two_ref
  65.0 0.0 collective-permute-done.12.three_ref
  65.0 0.8 %sum_rows.1 = bf16[128,1152]{1,0:T(8,128)(2,1)} custom-call(f32[128,1152]{1,0:T(8,128)S(1)} %get-tuple-element.54.keep_ref, bf16[128,1152]{1,0:T(8,128)(2,1)S(1)} %collective-permute-done.10.one_ref, bf16[128,1152]{1,0:T(8,128)(2,1)S(1)} %collective-permute-done.11.two_ref, bf16[128,1152]{1,0:T(8,128)(2,1)S(1)} %collective-permute-done.12.three_ref, ...), custom_call_target="tpu_custom_call" | custom-call | tf_op jit(solution)/shard_map/sum_devices/sum_rows/pallas_call | solution.py:367
  65.9 5.5 %all-to-all-start.2 = ((bf16[16,8,1152]{2,1,0:T(8,128)(2,1)}), bf16[16,8,1152]{2,1,0:T(8,128)(2,1)S(1)}, u32[]{:S(2)}, u32[]{:S(2)}) async-start(bf16[16,8,1152]{2,1,0:T(8,128)(2,1)} %bitcast.6), calls=%async_computation.2 | async-start | bytes 589824 | tf_op jit(solution)/shard_map/sum_devices/all_to_all | solution.py:375
  71.4 1.8 %collective-permute-start.8 = (f32[8,1024]{1,0:T(8,128)S(1)}, f32[8,1024]{1,0:T(8,128)S(1)}, u32[]{:S(2)}, u32[]{:S(2)}) collective-permute-start(f32[8,1024]{1,0:T(8,128)S(1)} %get-tuple-element.52.after_ref), channel_id=1, source_target_pairs={{0,32},{32,64},{64,96},{96,0},{1,33},{33,65},{65,97},{97,1},{2,34}... | collective-permute-start | bytes 98312 | tf_op jit(solution)/shard_map/sum_devices/ppermute | solution.py:366
  73.2 2.4 %collective-permute-start.7 = (f32[8,1024]{1,0:T(8,128)S(1)}, f32[8,1024]{1,0:T(8,128)S(1)}, u32[]{:S(2)}, u32[]{:S(2)}) collective-permute-start(f32[8,1024]{1,0:T(8,128)S(1)} %get-tuple-element.51), channel_id=1, source_target_pairs={{0,64},{32,96},{64,0},{96,32},{1,65},{33,97},{65,1},{97,33},{2,66}... | collective-permute-start | bytes 98312 | tf_op jit(solution)/shard_map/sum_devices/ppermute | solution.py:366
  75.6 1.1 %collective-permute-start.9 = (f32[8,1024]{1,0:T(8,128)S(1)}, f32[8,1024]{1,0:T(8,128)S(1)}, u32[]{:S(2)}, u32[]{:S(2)}) collective-permute-start(f32[8,1024]{1,0:T(8,128)S(1)} %get-tuple-element.53), channel_id=1, source_target_pairs={{0,96},{32,0},{64,32},{96,64},{1,97},{33,1},{65,33},{97,65},{2,98}... | collective-permute-start | bytes 98312 | tf_op jit(solution)/shard_map/sum_devices/ppermute | solution.py:366
  76.6 1.9 %collective-permute-done.7.one_ref = f32[8,1024]{1,0:T(8,128)S(1)} collective-permute-done((f32[8,1024]{1,0:T(8,128)S(1)}, f32[8,1024]{1,0:T(8,128)S(1)}, u32[]{:S(2)}, u32[]{:S(2)}) %collective-permute-start.7) | collective-permute-done | bytes 32800 | tf_op jit(solution)/shard_map/sum_devices/ppermute | solution.py:366
  78.6 0.0 collective-permute-done.8.two_ref
  78.6 0.9 %collective-permute-done.9.three_ref = f32[8,1024]{1,0:T(8,128)S(1)} collective-permute-done((f32[8,1024]{1,0:T(8,128)S(1)}, f32[8,1024]{1,0:T(8,128)S(1)}, u32[]{:S(2)}, u32[]{:S(2)}) %collective-permute-start.9) | collective-permute-done | bytes 32800 | tf_op jit(solution)/shard_map/sum_devices/ppermute | solution.py:366
  79.5 0.6 all-to-all-done.2
  80.1 0.7 last_sums.1
Async XLA Ops:
  13.4 5.9 %copy-start = (bf16[1024,1024]{1,0:T(8,128)(2,1)S(1)}, bf16[1024,1024]{1,0:T(8,128)(2,1)}, u32[]{:S(2)}) copy-start(bf16[1024,1024]{1,0:T(8,128)(2,1)} %w_in_ref.1) | copy-start | bytes 6291460
  13.4 5.9 %copy-start.1 = (bf16[1024,1024]{1,0:T(8,128)(2,1)S(1)}, bf16[1024,1024]{1,0:T(8,128)(2,1)}, u32[]{:S(2)}) copy-start(bf16[1024,1024]{1,0:T(8,128)(2,1)} %w_mid_ref.3) | copy-start | bytes 6291460
  13.4 5.9 %copy-start.2 = (bf16[1024,128]{1,0:T(8,128)(2,1)S(1)}, bf16[1024,128]{1,0:T(8,128)(2,1)}, u32[]{:S(2)}) copy-start(bf16[1024,128]{1,0:T(8,128)(2,1)} %w_out_ref.1) | copy-start | bytes 786436
  13.4 5.9 %copy-start.3 = (s32[3,1024]{1,0:T(4,128)S(1)}, s32[3,1024]{1,0:T(4,128)}, u32[]{:S(2)}) copy-start(s32[3,1024]{1,0:T(4,128)} %seeds_ref.1) | copy-start | bytes 36868
  19.2 2.0 %collective-permute-start = (bf16[2048,128]{1,0:T(8,128)(2,1)S(1)}, bf16[2048,128]{1,0:T(8,128)(2,1)S(1)}, u32[]{:S(2)}, u32[]{:S(2)}) collective-permute-start(bf16[2048,128]{1,0:T(8,128)(2,1)S(1)} %get-tuple-element.35.after_ref), channel_id=1, source_target_pairs={{0,16},{16,0},{1,17},{17,1},{2,18},{18,2},{3,19},{19,3},{4,20},{20... | collective-permute-start | bytes 1572872 | tf_op jit(solution)/shard_map/exchange_grads/ppermute | solution.py:273
  21.3 10.0 %collective-permute-start.2 = (bf16[512,128]{1,0:T(8,128)(2,1)S(1)}, bf16[512,128]{1,0:T(8,128)(2,1)S(1)}, u32[]{:S(2)}, u32[]{:S(2)}) collective-permute-start(bf16[512,128]{1,0:T(8,128)(2,1)S(1)} %get-tuple-element.37.after_ref), channel_id=1, source_target_pairs={{0,32},{32,64},{64,96},{96,0},{1,33},{33,65},{65,97},{97,1},{2,34}... | collective-permute-start | bytes 393224 | tf_op jit(solution)/shard_map/exchange_grads/ppermute | solution.py:291
  21.9 9.3 %collective-permute-start.1 = (bf16[512,128]{1,0:T(8,128)(2,1)S(1)}, bf16[512,128]{1,0:T(8,128)(2,1)S(1)}, u32[]{:S(2)}, u32[]{:S(2)}) collective-permute-start(bf16[512,128]{1,0:T(8,128)(2,1)S(1)} %get-tuple-element.42), channel_id=1, source_target_pairs={{0,64},{32,96},{64,0},{96,32},{1,65},{33,97},{65,1},{97,33},{2,66}... | collective-permute-start | bytes 393224 | tf_op jit(solution)/shard_map/exchange_grads/ppermute | solution.py:291
  24.0 7.6 %collective-permute-start.3 = (bf16[512,128]{1,0:T(8,128)(2,1)S(1)}, bf16[512,128]{1,0:T(8,128)(2,1)S(1)}, u32[]{:S(2)}, u32[]{:S(2)}) collective-permute-start(bf16[512,128]{1,0:T(8,128)(2,1)S(1)} %get-tuple-element.43), channel_id=1, source_target_pairs={{0,96},{32,0},{64,32},{96,64},{1,97},{33,1},{65,33},{97,65},{2,98}... | collective-permute-start | bytes 393224 | tf_op jit(solution)/shard_map/exchange_grads/ppermute | solution.py:291
  31.1 2.8 %collective-permute-start.5 = (bf16[1024,512]{1,0:T(8,128)(2,1)S(1)}, bf16[1024,512]{1,0:T(8,128)(2,1)S(1)}, u32[]{:S(2)}, u32[]{:S(2)}) collective-permute-start(bf16[1024,512]{1,0:T(8,128)(2,1)S(1)} %get-tuple-element.48), channel_id=1, source_target_pairs={{0,16},{16,0},{1,17},{17,1},{2,18},{18,2},{3,19},{19,3},{4,20},{20... | collective-permute-start | bytes 3145736 | tf_op jit(solution)/shard_map/ppermute | solution.py:304
  32.0 3.5 %collective-permute-start.6 = (bf16[1152,512]{1,0:T(8,128)(2,1)S(1)}, bf16[1152,512]{1,0:T(8,128)(2,1)S(1)}, u32[]{:S(2)}, u32[]{:S(2)}) collective-permute-start(bf16[1152,512]{1,0:T(8,128)(2,1)S(1)} %delta_two.1.delta_two_ref.delta_ref), channel_id=1, source_target_pairs={{0,16},{16,0},{1,17},{17,1},{2,18},{18,2},{3,19},{19,3},{4,20},{20... | collective-permute-start | bytes 3538952 | tf_op jit(solution)/shard_map/backward/ppermute | solution.py:325
  33.6 3.8 %collective-permute-start.4 = (bf16[1024,512]{1,0:T(8,128)(2,1)S(1)}, bf16[1024,512]{1,0:T(8,128)(2,1)S(1)}, u32[]{:S(2)}, u32[]{:S(2)}) collective-permute-start(bf16[1024,512]{1,0:T(8,128)(2,1)S(1)} %delta_one.1.delta_ref), channel_id=1, source_target_pairs={{0,16},{16,0},{1,17},{17,1},{2,18},{18,2},{3,19},{19,3},{4,20},{20... | collective-permute-start | bytes 3145736 | tf_op jit(solution)/shard_map/backward/ppermute | solution.py:335
  39.6 25.1 %all-to-all-start.1 = ((bf16[16,32,1024]{2,1,0:T(8,128)(2,1)}), bf16[16,32,1024]{2,1,0:T(8,128)(2,1)S(1)}, u32[]{:S(2)}, u32[]{:S(2)}) async-start(bf16[16,32,1024]{2,1,0:T(8,128)(2,1)} %bitcast.4), calls=%async_computation.1 | async-start | bytes 2097152 | tf_op jit(solution)/shard_map/sum_devices/all_to_all | solution.py:356
  46.7 18.3 %collective-permute-start.11 = (bf16[128,1152]{1,0:T(8,128)(2,1)S(1)}, bf16[128,1152]{1,0:T(8,128)(2,1)S(1)}, u32[]{:S(2)}, u32[]{:S(2)}) collective-permute-start(bf16[128,1152]{1,0:T(8,128)(2,1)S(1)} %get-tuple-element.49.after_ref), channel_id=1, source_target_pairs={{0,32},{32,64},{64,96},{96,0},{1,33},{33,65},{65,97},{97,1},{2,34}... | collective-permute-start | bytes 884744 | tf_op jit(solution)/shard_map/sum_devices/ppermute | solution.py:347
  47.8 17.2 %collective-permute-start.10 = (bf16[128,1152]{1,0:T(8,128)(2,1)S(1)}, bf16[128,1152]{1,0:T(8,128)(2,1)S(1)}, u32[]{:S(2)}, u32[]{:S(2)}) collective-permute-start(bf16[128,1152]{1,0:T(8,128)(2,1)S(1)} %get-tuple-element.55), channel_id=1, source_target_pairs={{0,64},{32,96},{64,0},{96,32},{1,65},{33,97},{65,1},{97,33},{2,66}... | collective-permute-start | bytes 884744 | tf_op jit(solution)/shard_map/sum_devices/ppermute | solution.py:347
  50.0 15.0 %collective-permute-start.12 = (bf16[128,1152]{1,0:T(8,128)(2,1)S(1)}, bf16[128,1152]{1,0:T(8,128)(2,1)S(1)}, u32[]{:S(2)}, u32[]{:S(2)}) collective-permute-start(bf16[128,1152]{1,0:T(8,128)(2,1)S(1)} %get-tuple-element.56), channel_id=1, source_target_pairs={{0,96},{32,0},{64,32},{96,64},{1,97},{33,1},{65,33},{97,65},{2,98}... | collective-permute-start | bytes 884744 | tf_op jit(solution)/shard_map/sum_devices/ppermute | solution.py:347
  65.9 14.2 %all-to-all-start.2 = ((bf16[16,8,1152]{2,1,0:T(8,128)(2,1)}), bf16[16,8,1152]{2,1,0:T(8,128)(2,1)S(1)}, u32[]{:S(2)}, u32[]{:S(2)}) async-start(bf16[16,8,1152]{2,1,0:T(8,128)(2,1)} %bitcast.6), calls=%async_computation.2 | async-start | bytes 589824 | tf_op jit(solution)/shard_map/sum_devices/all_to_all | solution.py:375
  71.4 7.2 %collective-permute-start.8 = (f32[8,1024]{1,0:T(8,128)S(1)}, f32[8,1024]{1,0:T(8,128)S(1)}, u32[]{:S(2)}, u32[]{:S(2)}) collective-permute-start(f32[8,1024]{1,0:T(8,128)S(1)} %get-tuple-element.52.after_ref), channel_id=1, source_target_pairs={{0,32},{32,64},{64,96},{96,0},{1,33},{33,65},{65,97},{97,1},{2,34}... | collective-permute-start | bytes 98312 | tf_op jit(solution)/shard_map/sum_devices/ppermute | solution.py:366
  73.2 5.4 %collective-permute-start.7 = (f32[8,1024]{1,0:T(8,128)S(1)}, f32[8,1024]{1,0:T(8,128)S(1)}, u32[]{:S(2)}, u32[]{:S(2)}) collective-permute-start(f32[8,1024]{1,0:T(8,128)S(1)} %get-tuple-element.51), channel_id=1, source_target_pairs={{0,64},{32,96},{64,0},{96,32},{1,65},{33,97},{65,1},{97,33},{2,66}... | collective-permute-start | bytes 98312 | tf_op jit(solution)/shard_map/sum_devices/ppermute | solution.py:366
  75.6 3.9 %collective-permute-start.9 = (f32[8,1024]{1,0:T(8,128)S(1)}, f32[8,1024]{1,0:T(8,128)S(1)}, u32[]{:S(2)}, u32[]{:S(2)}) collective-permute-start(f32[8,1024]{1,0:T(8,128)S(1)} %get-tuple-element.53), channel_id=1, source_target_pairs={{0,96},{32,0},{64,32},{96,64},{1,97},{33,1},{65,33},{97,65},{2,98}... | collective-permute-start | bytes 98312 | tf_op jit(solution)/shard_map/sum_devices/ppermute | solution.py:366
where the time goes:
time: 81.1 us; the launch traced here: 80.7 us
  starting transfers between devices  27.6 us (34%)
  Pallas kernels  22.2 us (27%)
  waiting for transfers between devices  18.7 us (23%)
  blocking collectives  10.8 us (13%)
  between operations  1.47 us (2%)
    all_to_all x1, waiting for transfers between devices, per_device(): lax.all_to_all(out_one, ('x', 'y'), split_axis=0, concat_axis=0, tiled=True)  12.9 us
    all_to_all x1, blocking collectives, per_device(): lax.all_to_all(copies, ('z', 'core'), split_axis=0, concat_axis=0, tiled=...  10.8 us
    ppermute x6, starting transfers between devices, per_device(): lax.ppermute(pieces[step - 1], 'z', shift(step))  10.5 us
    all_to_all x1, starting transfers between devices, per_device(): lax.all_to_all(out_one, ('x', 'y'), split_axis=0, concat_axis=0, tiled=True)  7.04 us
    pallas_call x1, Pallas kernels, per_device(): pl.pallas_call(forward_kernel, out_shape=(shape((WIDTH, SHARE), F32),) *...  6.18 us
    pallas_call x1, Pallas kernels, per_device(): pl.pallas_call(segment_kernel, out_shape=(shape((2048, EMBED), F32), shap...  5.78 us
    all_to_all x1, starting transfers between devices, per_device(): lax.all_to_all(out_two, ('x', 'y'), split_axis=0, concat_axis=0, tiled=True)  5.53 us
    ppermute x3, starting transfers between devices, per_device(): lax.ppermute(part, 'z', shift(step))  3.69 us
  transfers between devices with their start and end apart: 15, of which 7 were waited for; matrix products, arithmetic and copies ran while one was open for 0% of the time, Pallas kernels for 14%

commit v1 on v0

--- a/solution.py
+++ b/solution.py
@@ -195,42 +195,46 @@
     for cols in TILES:
         total[:, cols] = over_slots(
             own_ref[512:1024, :], delta_ref[cols, :], got_ref[0:512, :], got_delta_ref[cols, :])
-    total[:, 1024:1152] = over_slots(
-        own_ref[1024:1536, :], delta_ref[1024:1152, :], got_ref[512:1024, :], got_delta_ref[1024:1152, :])
     z = lax.axis_index("z")
     for step, out_ref in enumerate((keep_ref, one_ref, two_ref, three_ref)):
         rows = pl.ds(pl.multiple_of(((z + step) & 3) * 128, 128), 128)
         out_ref[...] = total[rows, :].astype(out_ref.dtype)
 
 
-def weights_one_kernel(own_ref, delta_ref, other_ref, got_delta_ref, after_ref, out_ref):
+def by_column(value):
+    return jnp.concatenate([value[chip * 8 : chip * 8 + 8, :] for chip in BY_COLUMN], axis=0).astype(BF16)
+
+
+def weights_one_kernel(own_ref, delta_ref, other_ref, got_delta_ref, delta_two_ref, got_ref, got_delta_two_ref,
+                       after_ref, out_ref):
     for cols in TILES:
-        value = over_slots(own_ref[0:512, :], delta_ref[cols, :], other_ref[...], got_delta_ref[cols, :])
-        out_ref[:, cols] = jnp.concatenate(
-            [value[chip * 8 : chip * 8 + 8, :] for chip in BY_COLUMN], axis=0).astype(BF16)
-
-
-def sum_columns_kernel(pieces_ref, keep_ref, one_ref, two_ref, three_ref, total):
+        out_ref[:, cols] = by_column(
+            over_slots(own_ref[0:512, :], delta_ref[cols, :], other_ref[...], got_delta_ref[cols, :]))
+    out_ref[:, 1024:1152] = by_column(over_slots(
+        own_ref[1024:1536, :], delta_two_ref[1024:1152, :], got_ref[512:1024, :], got_delta_two_ref[1024:1152, :]))
+
+
+def sum_columns_kernel(pieces_ref, after_ref, keep_ref, one_ref, two_ref, three_ref, total):
     z = lax.axis_index("z")
-    for col in range(0, 1024, 128):
+    for col in range(0, 1152, 128):
         cols = slice(col, col + 128)
         total[:, cols] = sum(pieces_ref[piece * 32 : piece * 32 + 32, cols].astype(F32) for piece in range(16))
     for step, out_ref in enumerate((keep_ref, one_ref, two_ref, three_ref)):
         out_ref[...] = total[pl.ds(pl.multiple_of(((z + step) & 3) * 8, 8), 8), :]
 
 
-def sum_rows_kernel(keep_ref, one_ref, two_ref, three_ref, after_ref, out_ref):
+def sum_rows_kernel(keep_ref, one_ref, two_ref, three_ref, out_ref):
     total = keep_ref[...] + one_ref[...].astype(F32) + two_ref[...].astype(F32) + three_ref[...].astype(F32)
     out_ref[...] = total.astype(BF16)
 
 
 def last_kernel(keep_ref, one_ref, two_ref, three_ref, pieces_ref, in_ref, mid_ref, last_ref):
-    in_ref[...] = (keep_ref[...] + one_ref[...]) + (two_ref[...] + three_ref[...])
-    for start, out_ref in ((0, mid_ref), (1024, last_ref)):
-        for col in range(0, out_ref.shape[1], 128):
-            cols = slice(start + col, start + col + 128)
-            total = sum(pieces_ref[piece * 16 : piece * 16 + 16, cols].astype(F32) for piece in range(8))
-            out_ref[:, col : col + 128] = total[0:8, :] + total[8:16, :]
+    for cols, out_ref in ((slice(0, 1024), in_ref), (slice(1024, 1152), last_ref)):
+        out_ref[...] = (keep_ref[:, cols] + one_ref[:, cols]) + (two_ref[:, cols] + three_ref[:, cols])
+    for col in range(0, 1024, 128):
+        cols = slice(col, col + 128)
+        total = sum(pieces_ref[piece * 16 : piece * 16 + 16, cols].astype(F32) for piece in range(8))
+        mid_ref[:, cols] = total[0:8, :] + total[8:16, :]
 
 
 def shift(steps):
@@ -337,41 +341,41 @@
     with jax.named_scope("sum_devices"):
         keep_two, *pieces = pl.pallas_call(
             weights_two_kernel,
-            out_shape=(shape((128, 1152), F32),) + (shape((128, 1152), BF16),) * 3,
+            out_shape=(shape((128, 1024), F32),) + (shape((128, 1024), BF16),) * 3,
             in_specs=vmem(4),
             out_specs=tuple(vmem(4)),
-            scratch_shapes=[pltpu.VMEM((512, 1152), F32)],
+            scratch_shapes=[pltpu.VMEM((512, 1024), F32)],
             compiler_params=params(),
             name="weights_two",
         )(own_units, delta_two, got_units, got_delta_two)
         rows_two = [lax.ppermute(pieces[step - 1], "z", shift(step)) for step in (2, 1, 3)]
         out_one = pl.pallas_call(
             weights_one_kernel,
-            out_shape=shape((512, 1024), BF16),
-            in_specs=vmem(4) + [anywhere],
+            out_shape=shape((512, 1152), BF16),
+            in_specs=vmem(7) + [anywhere],
             out_specs=vmem(1)[0],
             compiler_params=params(),
             name="weights_one",
-        )(own_units, delta_one, other_enc, got_delta_one, pieces[0])
+        )(own_units, delta_one, other_enc, got_delta_one, delta_two, got_units, got_delta_two, pieces[0])
         columns_one = lax.all_to_all(out_one, ("x", "y"), split_axis=0, concat_axis=0, tiled=True)
+        out_two = pl.pallas_call(
+            sum_rows_kernel,
+            out_shape=shape((128, 1024), BF16),
+            in_specs=vmem(4),
+            out_specs=vmem(1)[0],
+            compiler_params=params(),
+            name="sum_rows",
+        )(keep_two, *rows_two)
         keep_one, *pieces = pl.pallas_call(
             sum_columns_kernel,
-            out_shape=(shape((8, 1024), F32),) * 4,
-            in_specs=vmem(1),
-            out_specs=tuple(vmem(4)),
-            scratch_shapes=[pltpu.VMEM((32, 1024), F32)],
+            out_shape=(shape((8, 1152), F32),) * 4,
+            in_specs=vmem(1) + [anywhere],
+            out_specs=tuple(vmem(4)),
+            scratch_shapes=[pltpu.VMEM((32, 1152), F32)],
             compiler_params=params(),
             name="sum_columns",
-        )(columns_one)
+        )(columns_one, out_two)
         rows_one = [lax.ppermute(pieces[step - 1], "z", shift(step)) for step in (2, 1, 3)]
-        out_two = pl.pallas_call(
-            sum_rows_kernel,
-            out_shape=shape((128, 1152), BF16),
-            in_specs=vmem(4) + [anywhere],
-            out_specs=vmem(1)[0],
-            compiler_params=params(),
-            name="sum_rows",
-        )(keep_two, *rows_two, pieces[0])
         columns_two = lax.all_to_all(out_two, ("x", "y"), split_axis=0, concat_axis=0, tiled=True)
         return pl.pallas_call(
             last_kernel,

time: 81.1 us -> 79.6 us (0.982)
  starting transfers between devices: 27.6 us -> 26.3 us
    all_to_all x1, waiting for transfers between devices: 12.9 us -> 3.2 us  [per_device(): lax.all_to_all(out_one, ('x', 'y'), split_axis=0, concat_axis=0, tiled=True)]
    ppermute x6, waiting for transfers between devices: 2.84 us -> 10.3 us  [per_device(): lax.ppermute(pieces[step - 1], 'z', shift(step))]
    all_to_all x1, waiting for transfers between devices: 0.59 us -> 2.44 us  [per_device(): lax.all_to_all(out_two, ('x', 'y'), split_axis=0, concat_axis=0, tiled=True)]
    all_to_all x1, starting transfers between devices: 5.53 us -> 3.68 us  [per_device(): lax.all_to_all(out_two, ('x', 'y'), split_axis=0, concat_axis=0, tiled=True)]
  transfers between devices with their start and end apart: 15 -> 15, of which waited for: 7 -> 7; matrix products, arithmetic and copies ran while one was open for 0% -> 0% of each run, Pallas kernels for 14% -> 15%
where the time goes in v1:
time: 79.6 us; the launch traced here: 79.2 us
  starting transfers between devices  26.3 us (33%)
  Pallas kernels  22.1 us (28%)
  waiting for transfers between devices  18.4 us (23%)
  blocking collectives  10.8 us (14%)
  between operations  1.44 us (2%)
    ppermute x6, starting transfers between devices, per_device(): lax.ppermute(pieces[step - 1], 'z', shift(step))  11.1 us
    all_to_all x1, blocking collectives, per_device(): lax.all_to_all(copies, ('z', 'core'), split_axis=0, concat_axis=0, tiled=...  10.8 us
    ppermute x6, waiting for transfers between devices, per_device(): lax.ppermute(pieces[step - 1], 'z', shift(step))  10.3 us
    all_to_all x1, starting transfers between devices, per_device(): lax.all_to_all(out_one, ('x', 'y'), split_axis=0, concat_axis=0, tiled=True)  7.04 us
    pallas_call x1, Pallas kernels, per_device(): pl.pallas_call(forward_kernel, out_shape=(shape((WIDTH, SHARE), F32),) *...  6.18 us
    pallas_call x1, Pallas kernels, per_device(): pl.pallas_call(segment_kernel, out_shape=(shape((2048, EMBED), F32), shap...  5.78 us
    ppermute x3, starting transfers between devices, per_device(): lax.ppermute(part, 'z', shift(step))  3.69 us
    all_to_all x1, starting transfers between devices, per_device(): lax.all_to_all(out_two, ('x', 'y'), split_axis=0, concat_axis=0, tiled=True)  3.68 us
  transfers between devices with their start and end apart: 15, of which 7 were waited for; matrix products, arithmetic and copies ran while one was open for 0% of the time, Pallas kernels for 15%

profile of v1, /device:TPU:0, one launch (start us, length us, event | category | flops | bytes accessed | tf_op | source)
XLA Modules:
  0.0 79.2 jit_solution(1733827520184401541)
XLA Ops:
  1.3 1.3 %pack_ids.1 = (s32[8,16,128]{2,1,0:T(8,128)S(1)}, bf16[4096,128]{1,0:T(8,128)(2,1)S(1)}, s32[32,128]{1,0:T(8,128)S(1)}, s32[32,128]{1,0:T(8,128)S(1)}) custom-call(s32[1]{0:T(128)S(6)} %copy.12.count_ref, s32[12,128]{1,0:T(8,128)} %bitcast.14, bf16[4096,128]{1,0:T(8,128)(2,1)} %cot_ref.1, s32[32,128]{1,0:T(8,128)} %bitcast.12, s32[32,128]{1,0:T(8,128)} %bitcast.13), custom_call_target="tpu_custom_call" | custom-call | tf_op jit(solution)/shard_map/gather_ids/pack_ids/pallas_call | solution.py:252
  2.6 10.8 %all_to_all.27 = s32[8,16,128]{2,1,0:T(8,128)S(1)} all-to-all(s32[8,16,128]{2,1,0:T(8,128)S(1)} %get-tuple-element.30), channel_id=1, replica_groups=mesh['z'=4,'core'=2,'x'=4,'y'=4] {'z','core'}, dimensions={0} | all-to-all | bytes 131072 | tf_op jit(solution)/shard_map/gather_ids/all_to_all | solution.py:263
  13.4 0.0 copy-start
  13.4 0.0 copy-start.1
  13.4 0.0 copy-start.2
  13.4 0.0 copy-start.3
  13.4 5.8 %segment_sums.1 = (f32[2048,128]{1,0:T(8,128)S(1)}, bf16[2048,128]{1,0:T(8,128)(2,1)S(1)}) custom-call(s32[128,128]{1,0:T(8,128)S(1)} %bitcast.10, s32[32,128]{1,0:T(8,128)S(1)} %get-tuple-element.31.row_ref, s32[32,128]{1,0:T(8,128)S(1)} %get-tuple-element.32.slot_ref, bf16[4096,128]{1,0:T(8,128)(2,1)S(1)} %get-tuple-element.33.cot_ref), custom_call_target="tpu_custom_call" | custom-call | flops 4294967296 | bytes 4194304 | tf_op jit(solution)/shard_map/segment_sums/pallas_call | solution.py:265
  19.2 0.1 collective-permute-start
  19.3 0.0 copy-done
  19.3 0.0 copy-done.1
  19.3 0.0 copy-done.2
  19.3 0.0 copy-done.3
  19.3 1.4 %transpose_weights.1 = (bf16[1024,1024]{1,0:T(8,128)(2,1)S(1)}, bf16[1024,1024]{1,0:T(8,128)(2,1)S(1)}, bf16[1024,128]{1,0:T(8,128)(2,1)S(1)}, s32[1024,8]{1,0:T(8,128)S(1)}) custom-call(bf16[1024,1024]{1,0:T(8,128)(2,1)S(1)} %copy-done, bf16[1024,1024]{1,0:T(8,128)(2,1)S(1)} %copy-done.1, bf16[1024,128]{1,0:T(8,128)(2,1)S(1)} %copy-done.2, ...), custom_call_target="tpu_custom_call" | custom-call | tf_op jit(solution)/shard_map/exchange_grads/transpose_weights/pallas_call | solution.py:278
  20.7 0.5 collective-permute-done.got_ref
  21.2 0.1 join_cores.1
  21.3 0.6 collective-permute-start.2
  21.9 2.1 %collective-permute-start.1 = (bf16[512,128]{1,0:T(8,128)(2,1)S(1)}, bf16[512,128]{1,0:T(8,128)(2,1)S(1)}, u32[]{:S(2)}, u32[]{:S(2)}) collective-permute-start(bf16[512,128]{1,0:T(8,128)(2,1)S(1)} %get-tuple-element.42), channel_id=1, source_target_pairs={{0,64},{32,96},{64,0},{96,32},{1,65},{33,97},{65,1},{97,33},{2,66}... | collective-permute-start | bytes 393224 | tf_op jit(solution)/shard_map/exchange_grads/ppermute | solution.py:295
  24.0 1.0 %collective-permute-start.3 = (bf16[512,128]{1,0:T(8,128)(2,1)S(1)}, bf16[512,128]{1,0:T(8,128)(2,1)S(1)}, u32[]{:S(2)}, u32[]{:S(2)}) collective-permute-start(bf16[512,128]{1,0:T(8,128)(2,1)S(1)} %get-tuple-element.43), channel_id=1, source_target_pairs={{0,96},{32,0},{64,32},{96,64},{1,97},{33,1},{65,33},{97,65},{2,98}... | collective-permute-start | bytes 393224 | tf_op jit(solution)/shard_map/exchange_grads/ppermute | solution.py:295
  25.0 6.2 %forward.1 = (f32[1024,512]{1,0:T(8,128)S(1)}, f32[1024,512]{1,0:T(8,128)S(1)}, bf16[1536,512]{1,0:T(8,128)(2,1)S(1)}, bf16[1024,512]{1,0:T(8,128)(2,1)S(1)}, bf16[512,512]{1,0:T(8,128)(2,1)S(1)}) custom-call(s32[128,128]{1,0:T(8,128)S(1)} %bitcast.11, bf16[512,128]{1,0:T(8,128)(2,1)S(1)} %get-tuple-element.37.after_ref, ...), custom_call_target="tpu_custom_call" | custom-call | flops 4294967296 | bytes 16777216 | tf_op jit(solution)/shard_map/forward/pallas_call | solution.py:297
  31.1 0.1 collective-permute-start.5
  31.2 0.0 collective-permute-done.2.two_ref
  31.2 0.0 collective-permute-done.1.one_ref
  31.3 0.3 collective-permute-done.3.three_ref
  31.5 0.1 total_grads.1.grad_ref
  31.6 0.4 delta_two.1.delta_two_ref.delta_ref
  32.0 0.3 collective-permute-start.6
  32.3 1.2 %delta_one.1.delta_ref = bf16[1024,512]{1,0:T(8,128)(2,1)S(1)} custom-call(bf16[1152,512]{1,0:T(8,128)(2,1)S(1)} %delta_two.1.delta_two_ref.delta_ref, f32[1024,512]{1,0:T(8,128)S(1)} %get-tuple-element.46.slope_ref, bf16[1024,1024]{1,0:T(8,128)(2,1)S(1)} %copy-done.1), custom_call_target="tpu_custom_call" | custom-call | flops 21474836480 | bytes 33554432 | tf_op jit(solution)/shard_map/backward/delta_one/pallas_call | solution.py:330
  33.6 0.4 collective-permute-start.4
  33.9 0.0 collective-permute-done.5.got_ref
  33.9 1.6 %collective-permute-done.6.got_delta_ref.got_delta_two_ref = bf16[1152,512]{1,0:T(8,128)(2,1)S(1)} collective-permute-done((bf16[1152,512]{1,0:T(8,128)(2,1)S(1)}, bf16[1152,512]{1,0:T(8,128)(2,1)S(1)}, u32[]{:S(2)}, u32[]{:S(2)}) %collective-permute-start.6) | collective-permute-done | bytes 1179680 | tf_op jit(solution)/shard_map/backward/ppermute | solution.py:329
  35.6 1.5 %weights_two.1 = (f32[128,1024]{1,0:T(8,128)S(1)}, bf16[128,1024]{1,0:T(8,128)(2,1)S(1)}, bf16[128,1024]{1,0:T(8,128)(2,1)S(1)}, bf16[128,1024]{1,0:T(8,128)(2,1)S(1)}) custom-call(bf16[1536,512]{1,0:T(8,128)(2,1)S(1)} %get-tuple-element.40.after_ref.own_ref, bf16[1152,512]{1,0:T(8,128)(2,1)S(1)} %delta_two.1.delta_two_ref.delta_ref, ...), custom_call_target="tpu_custom_call" | custom-call | tf_op jit(solution)/shard_map/sum_devices/weights_two/pallas_call | solution.py:342
  37.0 0.0 collective-permute-done.4.got_delta_ref
  37.1 2.6 %weights_one.1 = bf16[512,1152]{1,0:T(8,128)(2,1)} custom-call(bf16[1536,512]{1,0:T(8,128)(2,1)S(1)} %get-tuple-element.40.after_ref.own_ref, bf16[1024,512]{1,0:T(8,128)(2,1)S(1)} %delta_one.1.delta_ref, bf16[512,512]{1,0:T(8,128)(2,1)S(1)} %get-tuple-element.47.other_ref, bf16[1024,512]{1,0:T(8,128)(2,1)S(1)} %collective-permute-done.4.got_delta_ref, ...), custom_call_target="tpu_custom_call" | custom-call | tf_op jit(solution)/shard_map/sum_devices/weights_one/pallas_call | solution.py:352
  39.7 7.0 %all-to-all-start.1 = ((bf16[16,32,1152]{2,1,0:T(8,128)(2,1)}), bf16[16,32,1152]{2,1,0:T(8,128)(2,1)S(1)}, u32[]{:S(2)}, u32[]{:S(2)}) async-start(bf16[16,32,1152]{2,1,0:T(8,128)(2,1)} %bitcast.4), calls=%async_computation.1 | async-start | bytes 2359296 | tf_op jit(solution)/shard_map/sum_devices/all_to_all | solution.py:360
  46.7 1.1 %collective-permute-start.8 = (bf16[128,1024]{1,0:T(8,128)(2,1)S(1)}, bf16[128,1024]{1,0:T(8,128)(2,1)S(1)}, u32[]{:S(2)}, u32[]{:S(2)}) collective-permute-start(bf16[128,1024]{1,0:T(8,128)(2,1)S(1)} %get-tuple-element.49.after_ref), channel_id=1, source_target_pairs={{0,32},{32,64},{64,96},{96,0},{1,33},{33,65},{65,97},{97,1},{2,34}... | collective-permute-start | bytes 786440 | tf_op jit(solution)/shard_map/sum_devices/ppermute | solution.py:351
  47.8 2.2 %collective-permute-start.7 = (bf16[128,1024]{1,0:T(8,128)(2,1)S(1)}, bf16[128,1024]{1,0:T(8,128)(2,1)S(1)}, u32[]{:S(2)}, u32[]{:S(2)}) collective-permute-start(bf16[128,1024]{1,0:T(8,128)(2,1)S(1)} %get-tuple-element.51), channel_id=1, source_target_pairs={{0,64},{32,96},{64,0},{96,32},{1,65},{33,97},{65,1},{97,33},{2,66}... | collective-permute-start | bytes 786440 | tf_op jit(solution)/shard_map/sum_devices/ppermute | solution.py:351
  50.1 1.9 %collective-permute-start.9 = (bf16[128,1024]{1,0:T(8,128)(2,1)S(1)}, bf16[128,1024]{1,0:T(8,128)(2,1)S(1)}, u32[]{:S(2)}, u32[]{:S(2)}) collective-permute-start(bf16[128,1024]{1,0:T(8,128)(2,1)S(1)} %get-tuple-element.52), channel_id=1, source_target_pairs={{0,96},{32,0},{64,32},{96,64},{1,97},{33,1},{65,33},{97,65},{2,98}... | collective-permute-start | bytes 786440 | tf_op jit(solution)/shard_map/sum_devices/ppermute | solution.py:351
  52.0 9.8 %collective-permute-done.7.one_ref = bf16[128,1024]{1,0:T(8,128)(2,1)S(1)} collective-permute-done((bf16[128,1024]{1,0:T(8,128)(2,1)S(1)}, bf16[128,1024]{1,0:T(8,128)(2,1)S(1)}, u32[]{:S(2)}, u32[]{:S(2)}) %collective-permute-start.7) | collective-permute-done | bytes 262176 | tf_op jit(solution)/shard_map/sum_devices/ppermute | solution.py:351
  61.7 0.0 collective-permute-done.8.two_ref
  61.7 0.6 collective-permute-done.9.three_ref
  62.3 0.8 %sum_rows.1.after_ref = bf16[128,1024]{1,0:T(8,128)(2,1)} custom-call(f32[128,1024]{1,0:T(8,128)S(1)} %get-tuple-element.50.keep_ref, bf16[128,1024]{1,0:T(8,128)(2,1)S(1)} %collective-permute-done.7.one_ref, bf16[128,1024]{1,0:T(8,128)(2,1)S(1)} %collective-permute-done.8.two_ref, bf16[128,1024]{1,0:T(8,128)(2,1)S(1)} %collective-permute-done.9.three_ref), custom_call_target="tpu_custom_call" | custom-call | tf_op jit(solution)/shard_map/sum_devices/sum_rows/pallas_call | solution.py:361
  63.1 3.2 %all-to-all-done.1 = bf16[16,32,1152]{2,1,0:T(8,128)(2,1)S(1)} async-done(((bf16[16,32,1152]{2,1,0:T(8,128)(2,1)}), bf16[16,32,1152]{2,1,0:T(8,128)(2,1)S(1)}, u32[]{:S(2)}, u32[]{:S(2)}) %all-to-all-start.1) | async-done | bytes 1179680 | tf_op jit(solution)/shard_map/sum_devices/all_to_all | solution.py:360
  66.3 3.7 %all-to-all-start.2 = ((bf16[16,8,1024]{2,1,0:T(8,128)(2,1)}), bf16[16,8,1024]{2,1,0:T(8,128)(2,1)S(1)}, u32[]{:S(2)}, u32[]{:S(2)}) async-start(bf16[16,8,1024]{2,1,0:T(8,128)(2,1)} %bitcast.6), calls=%async_computation.2 | async-start | bytes 524288 | tf_op jit(solution)/shard_map/sum_devices/all_to_all | solution.py:379
  70.0 0.2 sum_columns.1
  70.2 2.6 %collective-permute-start.10 = (f32[8,1152]{1,0:T(8,128)S(1)}, f32[8,1152]{1,0:T(8,128)S(1)}, u32[]{:S(2)}, u32[]{:S(2)}) collective-permute-start(f32[8,1152]{1,0:T(8,128)S(1)} %get-tuple-element.54), channel_id=1, source_target_pairs={{0,64},{32,96},{64,0},{96,32},{1,65},{33,97},{65,1},{97,33},{2,66}... | collective-permute-start | bytes 110600 | tf_op jit(solution)/shard_map/sum_devices/ppermute | solution.py:378
  72.8 0.9 %collective-permute-start.11 = (f32[8,1152]{1,0:T(8,128)S(1)}, f32[8,1152]{1,0:T(8,128)S(1)}, u32[]{:S(2)}, u32[]{:S(2)}) collective-permute-start(f32[8,1152]{1,0:T(8,128)S(1)} %get-tuple-element.55), channel_id=1, source_target_pairs={{0,32},{32,64},{64,96},{96,0},{1,33},{33,65},{65,97},{97,1},{2,34}... | collective-permute-start | bytes 110600 | tf_op jit(solution)/shard_map/sum_devices/ppermute | solution.py:378
  73.7 2.3 %collective-permute-start.12 = (f32[8,1152]{1,0:T(8,128)S(1)}, f32[8,1152]{1,0:T(8,128)S(1)}, u32[]{:S(2)}, u32[]{:S(2)}) collective-permute-start(f32[8,1152]{1,0:T(8,128)S(1)} %get-tuple-element.56), channel_id=1, source_target_pairs={{0,96},{32,0},{64,32},{96,64},{1,97},{33,1},{65,33},{97,65},{2,98}... | collective-permute-start | bytes 110600 | tf_op jit(solution)/shard_map/sum_devices/ppermute | solution.py:378
  76.0 2.4 %all-to-all-done.2 = bf16[16,8,1024]{2,1,0:T(8,128)(2,1)S(1)} async-done(((bf16[16,8,1024]{2,1,0:T(8,128)(2,1)}), bf16[16,8,1024]{2,1,0:T(8,128)(2,1)S(1)}, u32[]{:S(2)}, u32[]{:S(2)}) %all-to-all-start.2) | async-done | bytes 262176 | tf_op jit(solution)/shard_map/sum_devices/all_to_all | solution.py:379
  78.5 0.0 collective-permute-done.10.one_ref
  78.5 0.0 collective-permute-done.11.two_ref
  78.5 0.0 collective-permute-done.12.three_ref
  78.5 0.7 last_sums.1
Async XLA Ops:
  13.4 5.9 %copy-start = (bf16[1024,1024]{1,0:T(8,128)(2,1)S(1)}, bf16[1024,1024]{1,0:T(8,128)(2,1)}, u32[]{:S(2)}) copy-start(bf16[1024,1024]{1,0:T(8,128)(2,1)} %w_in_ref.1) | copy-start | bytes 6291460
  13.4 5.9 %copy-start.1 = (bf16[1024,1024]{1,0:T(8,128)(2,1)S(1)}, bf16[1024,1024]{1,0:T(8,128)(2,1)}, u32[]{:S(2)}) copy-start(bf16[1024,1024]{1,0:T(8,128)(2,1)} %w_mid_ref.3) | copy-start | bytes 6291460
  13.4 5.9 %copy-start.2 = (bf16[1024,128]{1,0:T(8,128)(2,1)S(1)}, bf16[1024,128]{1,0:T(8,128)(2,1)}, u32[]{:S(2)}) copy-start(bf16[1024,128]{1,0:T(8,128)(2,1)} %w_out_ref.1) | copy-start | bytes 786436
  13.4 5.9 %copy-start.3 = (s32[3,1024]{1,0:T(4,128)S(1)}, s32[3,1024]{1,0:T(4,128)}, u32[]{:S(2)}) copy-start(s32[3,1024]{1,0:T(4,128)} %seeds_ref.1) | copy-start | bytes 36868
  19.2 2.0 %collective-permute-start = (bf16[2048,128]{1,0:T(8,128)(2,1)S(1)}, bf16[2048,128]{1,0:T(8,128)(2,1)S(1)}, u32[]{:S(2)}, u32[]{:S(2)}) collective-permute-start(bf16[2048,128]{1,0:T(8,128)(2,1)S(1)} %get-tuple-element.35.after_ref), channel_id=1, source_target_pairs={{0,16},{16,0},{1,17},{17,1},{2,18},{18,2},{3,19},{19,3},{4,20},{20... | collective-permute-start | bytes 1572872 | tf_op jit(solution)/shard_map/exchange_grads/ppermute | solution.py:277
  21.3 10.0 %collective-permute-start.2 = (bf16[512,128]{1,0:T(8,128)(2,1)S(1)}, bf16[512,128]{1,0:T(8,128)(2,1)S(1)}, u32[]{:S(2)}, u32[]{:S(2)}) collective-permute-start(bf16[512,128]{1,0:T(8,128)(2,1)S(1)} %get-tuple-element.37.after_ref), channel_id=1, source_target_pairs={{0,32},{32,64},{64,96},{96,0},{1,33},{33,65},{65,97},{97,1},{2,34}... | collective-permute-start | bytes 393224 | tf_op jit(solution)/shard_map/exchange_grads/ppermute | solution.py:295
  21.9 9.3 %collective-permute-start.1 = (bf16[512,128]{1,0:T(8,128)(2,1)S(1)}, bf16[512,128]{1,0:T(8,128)(2,1)S(1)}, u32[]{:S(2)}, u32[]{:S(2)}) collective-permute-start(bf16[512,128]{1,0:T(8,128)(2,1)S(1)} %get-tuple-element.42), channel_id=1, source_target_pairs={{0,64},{32,96},{64,0},{96,32},{1,65},{33,97},{65,1},{97,33},{2,66}... | collective-permute-start | bytes 393224 | tf_op jit(solution)/shard_map/exchange_grads/ppermute | solution.py:295
  24.0 7.6 %collective-permute-start.3 = (bf16[512,128]{1,0:T(8,128)(2,1)S(1)}, bf16[512,128]{1,0:T(8,128)(2,1)S(1)}, u32[]{:S(2)}, u32[]{:S(2)}) collective-permute-start(bf16[512,128]{1,0:T(8,128)(2,1)S(1)} %get-tuple-element.43), channel_id=1, source_target_pairs={{0,96},{32,0},{64,32},{96,64},{1,97},{33,1},{65,33},{97,65},{2,98}... | collective-permute-start | bytes 393224 | tf_op jit(solution)/shard_map/exchange_grads/ppermute | solution.py:295
  31.1 2.8 %collective-permute-start.5 = (bf16[1024,512]{1,0:T(8,128)(2,1)S(1)}, bf16[1024,512]{1,0:T(8,128)(2,1)S(1)}, u32[]{:S(2)}, u32[]{:S(2)}) collective-permute-start(bf16[1024,512]{1,0:T(8,128)(2,1)S(1)} %get-tuple-element.48), channel_id=1, source_target_pairs={{0,16},{16,0},{1,17},{17,1},{2,18},{18,2},{3,19},{19,3},{4,20},{20... | collective-permute-start | bytes 3145736 | tf_op jit(solution)/shard_map/ppermute | solution.py:308
  32.0 3.5 %collective-permute-start.6 = (bf16[1152,512]{1,0:T(8,128)(2,1)S(1)}, bf16[1152,512]{1,0:T(8,128)(2,1)S(1)}, u32[]{:S(2)}, u32[]{:S(2)}) collective-permute-start(bf16[1152,512]{1,0:T(8,128)(2,1)S(1)} %delta_two.1.delta_two_ref.delta_ref), channel_id=1, source_target_pairs={{0,16},{16,0},{1,17},{17,1},{2,18},{18,2},{3,19},{19,3},{4,20},{20... | collective-permute-start | bytes 3538952 | tf_op jit(solution)/shard_map/backward/ppermute | solution.py:329
  33.6 3.5 %collective-permute-start.4 = (bf16[1024,512]{1,0:T(8,128)(2,1)S(1)}, bf16[1024,512]{1,0:T(8,128)(2,1)S(1)}, u32[]{:S(2)}, u32[]{:S(2)}) collective-permute-start(bf16[1024,512]{1,0:T(8,128)(2,1)S(1)} %delta_one.1.delta_ref), channel_id=1, source_target_pairs={{0,16},{16,0},{1,17},{17,1},{2,18},{18,2},{3,19},{19,3},{4,20},{20... | collective-permute-start | bytes 3145736 | tf_op jit(solution)/shard_map/backward/ppermute | solution.py:339
  39.7 26.6 %all-to-all-start.1 = ((bf16[16,32,1152]{2,1,0:T(8,128)(2,1)}), bf16[16,32,1152]{2,1,0:T(8,128)(2,1)S(1)}, u32[]{:S(2)}, u32[]{:S(2)}) async-start(bf16[16,32,1152]{2,1,0:T(8,128)(2,1)} %bitcast.4), calls=%async_computation.1 | async-start | bytes 2359296 | tf_op jit(solution)/shard_map/sum_devices/all_to_all | solution.py:360
  46.7 15.0 %collective-permute-start.8 = (bf16[128,1024]{1,0:T(8,128)(2,1)S(1)}, bf16[128,1024]{1,0:T(8,128)(2,1)S(1)}, u32[]{:S(2)}, u32[]{:S(2)}) collective-permute-start(bf16[128,1024]{1,0:T(8,128)(2,1)S(1)} %get-tuple-element.49.after_ref), channel_id=1, source_target_pairs={{0,32},{32,64},{64,96},{96,0},{1,33},{33,65},{65,97},{97,1},{2,34}... | collective-permute-start | bytes 786440 | tf_op jit(solution)/shard_map/sum_devices/ppermute | solution.py:351
  47.8 13.9 %collective-permute-start.7 = (bf16[128,1024]{1,0:T(8,128)(2,1)S(1)}, bf16[128,1024]{1,0:T(8,128)(2,1)S(1)}, u32[]{:S(2)}, u32[]{:S(2)}) collective-permute-start(bf16[128,1024]{1,0:T(8,128)(2,1)S(1)} %get-tuple-element.51), channel_id=1, source_target_pairs={{0,64},{32,96},{64,0},{96,32},{1,65},{33,97},{65,1},{97,33},{2,66}... | collective-permute-start | bytes 786440 | tf_op jit(solution)/shard_map/sum_devices/ppermute | solution.py:351
  50.1 12.2 %collective-permute-start.9 = (bf16[128,1024]{1,0:T(8,128)(2,1)S(1)}, bf16[128,1024]{1,0:T(8,128)(2,1)S(1)}, u32[]{:S(2)}, u32[]{:S(2)}) collective-permute-start(bf16[128,1024]{1,0:T(8,128)(2,1)S(1)} %get-tuple-element.52), channel_id=1, source_target_pairs={{0,96},{32,0},{64,32},{96,64},{1,97},{33,1},{65,33},{97,65},{2,98}... | collective-permute-start | bytes 786440 | tf_op jit(solution)/shard_map/sum_devices/ppermute | solution.py:351
  66.3 12.2 %all-to-all-start.2 = ((bf16[16,8,1024]{2,1,0:T(8,128)(2,1)}), bf16[16,8,1024]{2,1,0:T(8,128)(2,1)S(1)}, u32[]{:S(2)}, u32[]{:S(2)}) async-start(bf16[16,8,1024]{2,1,0:T(8,128)(2,1)} %bitcast.6), calls=%async_computation.2 | async-start | bytes 524288 | tf_op jit(solution)/shard_map/sum_devices/all_to_all | solution.py:379
  70.2 8.3 %collective-permute-start.10 = (f32[8,1152]{1,0:T(8,128)S(1)}, f32[8,1152]{1,0:T(8,128)S(1)}, u32[]{:S(2)}, u32[]{:S(2)}) collective-permute-start(f32[8,1152]{1,0:T(8,128)S(1)} %get-tuple-element.54), channel_id=1, source_target_pairs={{0,64},{32,96},{64,0},{96,32},{1,65},{33,97},{65,1},{97,33},{2,66}... | collective-permute-start | bytes 110600 | tf_op jit(solution)/shard_map/sum_devices/ppermute | solution.py:378
  72.8 5.7 %collective-permute-start.11 = (f32[8,1152]{1,0:T(8,128)S(1)}, f32[8,1152]{1,0:T(8,128)S(1)}, u32[]{:S(2)}, u32[]{:S(2)}) collective-permute-start(f32[8,1152]{1,0:T(8,128)S(1)} %get-tuple-element.55), channel_id=1, source_target_pairs={{0,32},{32,64},{64,96},{96,0},{1,33},{33,65},{65,97},{97,1},{2,34}... | collective-permute-start | bytes 110600 | tf_op jit(solution)/shard_map/sum_devices/ppermute | solution.py:378
  73.7 4.7 %collective-permute-start.12 = (f32[8,1152]{1,0:T(8,128)S(1)}, f32[8,1152]{1,0:T(8,128)S(1)}, u32[]{:S(2)}, u32[]{:S(2)}) collective-permute-start(f32[8,1152]{1,0:T(8,128)S(1)} %get-tuple-element.56), channel_id=1, source_target_pairs={{0,96},{32,0},{64,32},{96,64},{1,97},{33,1},{65,33},{97,65},{2,98}... | collective-permute-start | bytes 110600 | tf_op jit(solution)/shard_map/sum_devices/ppermute | solution.py:378

commit v2 on v1

--- a/solution.py
+++ b/solution.py
@@ -206,12 +206,22 @@
 
 
 def weights_one_kernel(own_ref, delta_ref, other_ref, got_delta_ref, delta_two_ref, got_ref, got_delta_two_ref,
-                       after_ref, out_ref):
+                       after_ref, out_ref, tiles, sems):
+    copies = []
+
+    def leave(cols):
+        copies.append(pltpu.make_async_copy(tiles.at[:, cols], out_ref.at[:, cols], sems.at[len(copies)]))
+        copies[-1].start()
+
+    tiles[:, 1024:1152] = by_column(over_slots(
+        own_ref[1024:1536, :], delta_two_ref[1024:1152, :], got_ref[512:1024, :], got_delta_two_ref[1024:1152, :]))
+    leave(slice(1024, 1152))
     for cols in TILES:
-        out_ref[:, cols] = by_column(
+        tiles[:, cols] = by_column(
             over_slots(own_ref[0:512, :], delta_ref[cols, :], other_ref[...], got_delta_ref[cols, :]))
-    out_ref[:, 1024:1152] = by_column(over_slots(
-        own_ref[1024:1536, :], delta_two_ref[1024:1152, :], got_ref[512:1024, :], got_delta_two_ref[1024:1152, :]))
+        leave(cols)
+    for copy in copies:
+        copy.wait()
 
 
 def sum_columns_kernel(pieces_ref, after_ref, keep_ref, one_ref, two_ref, three_ref, total):
@@ -353,7 +363,8 @@
             weights_one_kernel,
             out_shape=shape((512, 1152), BF16),
             in_specs=vmem(7) + [anywhere],
-            out_specs=vmem(1)[0],
+            out_specs=anywhere,
+            scratch_shapes=[pltpu.VMEM((512, 1152), BF16), pltpu.SemaphoreType.DMA((5,))],
             compiler_params=params(),
             name="weights_one",
         )(own_units, delta_one, other_enc, got_delta_one, delta_two, got_units, got_delta_two, pieces[0])

time: 79.6 us -> 79.5 us (level)
  no operation moved by 1% of the time
where the time goes in v2:
time: 79.5 us; the launch traced here: 79 us
  starting transfers between devices  26.4 us (33%)
  Pallas kernels  22 us (28%)
  waiting for transfers between devices  18.4 us (23%)
  blocking collectives  10.8 us (14%)
  between operations  1.45 us (2%)
    ppermute x6, starting transfers between devices, per_device(): lax.ppermute(pieces[step - 1], 'z', shift(step))  11.1 us
    all_to_all x1, blocking collectives, per_device(): lax.all_to_all(copies, ('z', 'core'), split_axis=0, concat_axis=0, tiled=...  10.8 us
    ppermute x6, waiting for transfers between devices, per_device(): lax.ppermute(pieces[step - 1], 'z', shift(step))  10.3 us
    all_to_all x1, starting transfers between devices, per_device(): lax.all_to_all(out_one, ('x', 'y'), split_axis=0, concat_axis=0, tiled=True)  7.05 us
    pallas_call x1, Pallas kernels, per_device(): pl.pallas_call(forward_kernel, out_shape=(shape((WIDTH, SHARE), F32),) *...  6.18 us
    pallas_call x1, Pallas kernels, per_device(): pl.pallas_call(segment_kernel, out_shape=(shape((2048, EMBED), F32), shap...  5.78 us
    ppermute x3, starting transfers between devices, per_device(): lax.ppermute(part, 'z', shift(step))  3.69 us
    all_to_all x1, starting transfers between devices, per_device(): lax.all_to_all(out_two, ('x', 'y'), split_axis=0, concat_axis=0, tiled=True)  3.68 us
  transfers between devices with their start and end apart: 15, of which 7 were waited for; matrix products, arithmetic and copies ran while one was open for 0% of the time, Pallas kernels for 15%

profile of v2, /device:TPU:0, one launch (start us, length us, event | category | flops | bytes accessed | tf_op | source)
XLA Modules:
  0.0 79.0 jit_solution(18244345756841494801)
XLA Ops:
  1.3 1.3 %pack_ids.1 = (s32[8,16,128]{2,1,0:T(8,128)S(1)}, bf16[4096,128]{1,0:T(8,128)(2,1)S(1)}, s32[32,128]{1,0:T(8,128)S(1)}, s32[32,128]{1,0:T(8,128)S(1)}) custom-call(s32[1]{0:T(128)S(6)} %copy.12.count_ref, s32[12,128]{1,0:T(8,128)} %bitcast.14, bf16[4096,128]{1,0:T(8,128)(2,1)} %cot_ref.1, s32[32,128]{1,0:T(8,128)} %bitcast.12, s32[32,128]{1,0:T(8,128)} %bitcast.13), custom_call_target="tpu_custom_call" | custom-call | tf_op jit(solution)/shard_map/gather_ids/pack_ids/pallas_call | solution.py:262
  2.6 10.8 %all_to_all.27 = s32[8,16,128]{2,1,0:T(8,128)S(1)} all-to-all(s32[8,16,128]{2,1,0:T(8,128)S(1)} %get-tuple-element.30), channel_id=1, replica_groups=mesh['z'=4,'core'=2,'x'=4,'y'=4] {'z','core'}, dimensions={0} | all-to-all | bytes 131072 | tf_op jit(solution)/shard_map/gather_ids/all_to_all | solution.py:273
  13.4 0.0 copy-start
  13.4 0.0 copy-start.1
  13.4 0.0 copy-start.2
  13.4 0.0 copy-start.3
  13.4 5.8 %segment_sums.1 = (f32[2048,128]{1,0:T(8,128)S(1)}, bf16[2048,128]{1,0:T(8,128)(2,1)S(1)}) custom-call(s32[128,128]{1,0:T(8,128)S(1)} %bitcast.10, s32[32,128]{1,0:T(8,128)S(1)} %get-tuple-element.31.row_ref, s32[32,128]{1,0:T(8,128)S(1)} %get-tuple-element.32.slot_ref, bf16[4096,128]{1,0:T(8,128)(2,1)S(1)} %get-tuple-element.33.cot_ref), custom_call_target="tpu_custom_call" | custom-call | flops 4294967296 | bytes 4194304 | tf_op jit(solution)/shard_map/segment_sums/pallas_call | solution.py:275
  19.2 0.1 collective-permute-start
  19.3 0.0 copy-done
  19.3 0.0 copy-done.1
  19.3 0.0 copy-done.2
  19.3 0.0 copy-done.3
  19.3 1.4 %transpose_weights.1 = (bf16[1024,1024]{1,0:T(8,128)(2,1)S(1)}, bf16[1024,1024]{1,0:T(8,128)(2,1)S(1)}, bf16[1024,128]{1,0:T(8,128)(2,1)S(1)}, s32[1024,8]{1,0:T(8,128)S(1)}) custom-call(bf16[1024,1024]{1,0:T(8,128)(2,1)S(1)} %copy-done, bf16[1024,1024]{1,0:T(8,128)(2,1)S(1)} %copy-done.1, bf16[1024,128]{1,0:T(8,128)(2,1)S(1)} %copy-done.2, ...), custom_call_target="tpu_custom_call" | custom-call | tf_op jit(solution)/shard_map/exchange_grads/transpose_weights/pallas_call | solution.py:288
  20.7 0.5 collective-permute-done.got_ref
  21.2 0.1 join_cores.1
  21.3 0.6 collective-permute-start.2
  21.9 2.1 %collective-permute-start.1 = (bf16[512,128]{1,0:T(8,128)(2,1)S(1)}, bf16[512,128]{1,0:T(8,128)(2,1)S(1)}, u32[]{:S(2)}, u32[]{:S(2)}) collective-permute-start(bf16[512,128]{1,0:T(8,128)(2,1)S(1)} %get-tuple-element.42), channel_id=1, source_target_pairs={{0,64},{32,96},{64,0},{96,32},{1,65},{33,97},{65,1},{97,33},{2,66}... | collective-permute-start | bytes 393224 | tf_op jit(solution)/shard_map/exchange_grads/ppermute | solution.py:305
  24.0 1.0 %collective-permute-start.3 = (bf16[512,128]{1,0:T(8,128)(2,1)S(1)}, bf16[512,128]{1,0:T(8,128)(2,1)S(1)}, u32[]{:S(2)}, u32[]{:S(2)}) collective-permute-start(bf16[512,128]{1,0:T(8,128)(2,1)S(1)} %get-tuple-element.43), channel_id=1, source_target_pairs={{0,96},{32,0},{64,32},{96,64},{1,97},{33,1},{65,33},{97,65},{2,98}... | collective-permute-start | bytes 393224 | tf_op jit(solution)/shard_map/exchange_grads/ppermute | solution.py:305
  25.0 6.2 %forward.1 = (f32[1024,512]{1,0:T(8,128)S(1)}, f32[1024,512]{1,0:T(8,128)S(1)}, bf16[1536,512]{1,0:T(8,128)(2,1)S(1)}, bf16[1024,512]{1,0:T(8,128)(2,1)S(1)}, bf16[512,512]{1,0:T(8,128)(2,1)S(1)}) custom-call(s32[128,128]{1,0:T(8,128)S(1)} %bitcast.11, bf16[512,128]{1,0:T(8,128)(2,1)S(1)} %get-tuple-element.37.after_ref, ...), custom_call_target="tpu_custom_call" | custom-call | flops 4294967296 | bytes 16777216 | tf_op jit(solution)/shard_map/forward/pallas_call | solution.py:307
  31.1 0.1 collective-permute-start.5
  31.2 0.0 collective-permute-done.2.two_ref
  31.2 0.0 collective-permute-done.1.one_ref
  31.3 0.3 collective-permute-done.3.three_ref
  31.5 0.1 total_grads.1.grad_ref
  31.6 0.4 delta_two.1.delta_two_ref.delta_ref
  32.0 0.3 collective-permute-start.6
  32.3 1.2 %delta_one.1.delta_ref = bf16[1024,512]{1,0:T(8,128)(2,1)S(1)} custom-call(bf16[1152,512]{1,0:T(8,128)(2,1)S(1)} %delta_two.1.delta_two_ref.delta_ref, f32[1024,512]{1,0:T(8,128)S(1)} %get-tuple-element.46.slope_ref, bf16[1024,1024]{1,0:T(8,128)(2,1)S(1)} %copy-done.1), custom_call_target="tpu_custom_call" | custom-call | flops 21474836480 | bytes 33554432 | tf_op jit(solution)/shard_map/backward/delta_one/pallas_call | solution.py:340
  33.6 0.4 collective-permute-start.4
  33.9 0.0 collective-permute-done.5.got_ref
  33.9 1.6 %collective-permute-done.6.got_delta_ref.got_delta_two_ref = bf16[1152,512]{1,0:T(8,128)(2,1)S(1)} collective-permute-done((bf16[1152,512]{1,0:T(8,128)(2,1)S(1)}, bf16[1152,512]{1,0:T(8,128)(2,1)S(1)}, u32[]{:S(2)}, u32[]{:S(2)}) %collective-permute-start.6) | collective-permute-done | bytes 1179680 | tf_op jit(solution)/shard_map/backward/ppermute | solution.py:339
  35.6 1.5 %weights_two.1 = (f32[128,1024]{1,0:T(8,128)S(1)}, bf16[128,1024]{1,0:T(8,128)(2,1)S(1)}, bf16[128,1024]{1,0:T(8,128)(2,1)S(1)}, bf16[128,1024]{1,0:T(8,128)(2,1)S(1)}) custom-call(bf16[1536,512]{1,0:T(8,128)(2,1)S(1)} %get-tuple-element.40.after_ref.own_ref, bf16[1152,512]{1,0:T(8,128)(2,1)S(1)} %delta_two.1.delta_two_ref.delta_ref, ...), custom_call_target="tpu_custom_call" | custom-call | tf_op jit(solution)/shard_map/sum_devices/weights_two/pallas_call | solution.py:352
  37.0 0.0 collective-permute-done.4.got_delta_ref
  37.1 2.5 %weights_one.1 = bf16[512,1152]{1,0:T(8,128)(2,1)} custom-call(bf16[1536,512]{1,0:T(8,128)(2,1)S(1)} %get-tuple-element.40.after_ref.own_ref, bf16[1024,512]{1,0:T(8,128)(2,1)S(1)} %delta_one.1.delta_ref, bf16[512,512]{1,0:T(8,128)(2,1)S(1)} %get-tuple-element.47.other_ref, bf16[1024,512]{1,0:T(8,128)(2,1)S(1)} %collective-permute-done.4.got_delta_ref, ...), custom_call_target="tpu_custom_call" | custom-call | tf_op jit(solution)/shard_map/sum_devices/weights_one/pallas_call | solution.py:362
  39.5 7.1 %all-to-all-start.1 = ((bf16[16,32,1152]{2,1,0:T(8,128)(2,1)}), bf16[16,32,1152]{2,1,0:T(8,128)(2,1)S(1)}, u32[]{:S(2)}, u32[]{:S(2)}) async-start(bf16[16,32,1152]{2,1,0:T(8,128)(2,1)} %bitcast.4), calls=%async_computation.1 | async-start | bytes 2359296 | tf_op jit(solution)/shard_map/sum_devices/all_to_all | solution.py:371
  46.6 1.1 %collective-permute-start.8 = (bf16[128,1024]{1,0:T(8,128)(2,1)S(1)}, bf16[128,1024]{1,0:T(8,128)(2,1)S(1)}, u32[]{:S(2)}, u32[]{:S(2)}) collective-permute-start(bf16[128,1024]{1,0:T(8,128)(2,1)S(1)} %get-tuple-element.49.after_ref), channel_id=1, source_target_pairs={{0,32},{32,64},{64,96},{96,0},{1,33},{33,65},{65,97},{97,1},{2,34}... | collective-permute-start | bytes 786440 | tf_op jit(solution)/shard_map/sum_devices/ppermute | solution.py:361
  47.7 2.2 %collective-permute-start.7 = (bf16[128,1024]{1,0:T(8,128)(2,1)S(1)}, bf16[128,1024]{1,0:T(8,128)(2,1)S(1)}, u32[]{:S(2)}, u32[]{:S(2)}) collective-permute-start(bf16[128,1024]{1,0:T(8,128)(2,1)S(1)} %get-tuple-element.51), channel_id=1, source_target_pairs={{0,64},{32,96},{64,0},{96,32},{1,65},{33,97},{65,1},{97,33},{2,66}... | collective-permute-start | bytes 786440 | tf_op jit(solution)/shard_map/sum_devices/ppermute | solution.py:361
  49.9 1.9 %collective-permute-start.9 = (bf16[128,1024]{1,0:T(8,128)(2,1)S(1)}, bf16[128,1024]{1,0:T(8,128)(2,1)S(1)}, u32[]{:S(2)}, u32[]{:S(2)}) collective-permute-start(bf16[128,1024]{1,0:T(8,128)(2,1)S(1)} %get-tuple-element.52), channel_id=1, source_target_pairs={{0,96},{32,0},{64,32},{96,64},{1,97},{33,1},{65,33},{97,65},{2,98}... | collective-permute-start | bytes 786440 | tf_op jit(solution)/shard_map/sum_devices/ppermute | solution.py:361
  51.8 9.8 %collective-permute-done.7.one_ref = bf16[128,1024]{1,0:T(8,128)(2,1)S(1)} collective-permute-done((bf16[128,1024]{1,0:T(8,128)(2,1)S(1)}, bf16[128,1024]{1,0:T(8,128)(2,1)S(1)}, u32[]{:S(2)}, u32[]{:S(2)}) %collective-permute-start.7) | collective-permute-done | bytes 262176 | tf_op jit(solution)/shard_map/sum_devices/ppermute | solution.py:361
  61.6 0.0 collective-permute-done.8.two_ref
  61.6 0.6 collective-permute-done.9.three_ref
  62.2 0.8 %sum_rows.1.after_ref = bf16[128,1024]{1,0:T(8,128)(2,1)} custom-call(f32[128,1024]{1,0:T(8,128)S(1)} %get-tuple-element.50.keep_ref, bf16[128,1024]{1,0:T(8,128)(2,1)S(1)} %collective-permute-done.7.one_ref, bf16[128,1024]{1,0:T(8,128)(2,1)S(1)} %collective-permute-done.8.two_ref, bf16[128,1024]{1,0:T(8,128)(2,1)S(1)} %collective-permute-done.9.three_ref), custom_call_target="tpu_custom_call" | custom-call | tf_op jit(solution)/shard_map/sum_devices/sum_rows/pallas_call | solution.py:372
  63.0 3.2 %all-to-all-done.1 = bf16[16,32,1152]{2,1,0:T(8,128)(2,1)S(1)} async-done(((bf16[16,32,1152]{2,1,0:T(8,128)(2,1)}), bf16[16,32,1152]{2,1,0:T(8,128)(2,1)S(1)}, u32[]{:S(2)}, u32[]{:S(2)}) %all-to-all-start.1) | async-done | bytes 1179680 | tf_op jit(solution)/shard_map/sum_devices/all_to_all | solution.py:371
  66.2 3.7 %all-to-all-start.2 = ((bf16[16,8,1024]{2,1,0:T(8,128)(2,1)}), bf16[16,8,1024]{2,1,0:T(8,128)(2,1)S(1)}, u32[]{:S(2)}, u32[]{:S(2)}) async-start(bf16[16,8,1024]{2,1,0:T(8,128)(2,1)} %bitcast.6), calls=%async_computation.2 | async-start | bytes 524288 | tf_op jit(solution)/shard_map/sum_devices/all_to_all | solution.py:390
  69.9 0.2 sum_columns.1
  70.0 2.6 %collective-permute-start.10 = (f32[8,1152]{1,0:T(8,128)S(1)}, f32[8,1152]{1,0:T(8,128)S(1)}, u32[]{:S(2)}, u32[]{:S(2)}) collective-permute-start(f32[8,1152]{1,0:T(8,128)S(1)} %get-tuple-element.54), channel_id=1, source_target_pairs={{0,64},{32,96},{64,0},{96,32},{1,65},{33,97},{65,1},{97,33},{2,66}... | collective-permute-start | bytes 110600 | tf_op jit(solution)/shard_map/sum_devices/ppermute | solution.py:389
  72.7 0.9 %collective-permute-start.11 = (f32[8,1152]{1,0:T(8,128)S(1)}, f32[8,1152]{1,0:T(8,128)S(1)}, u32[]{:S(2)}, u32[]{:S(2)}) collective-permute-start(f32[8,1152]{1,0:T(8,128)S(1)} %get-tuple-element.55), channel_id=1, source_target_pairs={{0,32},{32,64},{64,96},{96,0},{1,33},{33,65},{65,97},{97,1},{2,34}... | collective-permute-start | bytes 110600 | tf_op jit(solution)/shard_map/sum_devices/ppermute | solution.py:389
  73.6 2.3 %collective-permute-start.12 = (f32[8,1152]{1,0:T(8,128)S(1)}, f32[8,1152]{1,0:T(8,128)S(1)}, u32[]{:S(2)}, u32[]{:S(2)}) collective-permute-start(f32[8,1152]{1,0:T(8,128)S(1)} %get-tuple-element.56), channel_id=1, source_target_pairs={{0,96},{32,0},{64,32},{96,64},{1,97},{33,1},{65,33},{97,65},{2,98}... | collective-permute-start | bytes 110600 | tf_op jit(solution)/shard_map/sum_devices/ppermute | solution.py:389
  75.9 2.4 %all-to-all-done.2 = bf16[16,8,1024]{2,1,0:T(8,128)(2,1)S(1)} async-done(((bf16[16,8,1024]{2,1,0:T(8,128)(2,1)}), bf16[16,8,1024]{2,1,0:T(8,128)(2,1)S(1)}, u32[]{:S(2)}, u32[]{:S(2)}) %all-to-all-start.2) | async-done | bytes 262176 | tf_op jit(solution)/shard_map/sum_devices/all_to_all | solution.py:390
  78.3 0.0 collective-permute-done.10.one_ref
  78.4 0.0 collective-permute-done.11.two_ref
  78.4 0.0 collective-permute-done.12.three_ref
  78.4 0.7 last_sums.1
Async XLA Ops:
  13.4 5.9 %copy-start = (bf16[1024,1024]{1,0:T(8,128)(2,1)S(1)}, bf16[1024,1024]{1,0:T(8,128)(2,1)}, u32[]{:S(2)}) copy-start(bf16[1024,1024]{1,0:T(8,128)(2,1)} %w_in_ref.1) | copy-start | bytes 6291460
  13.4 5.9 %copy-start.1 = (bf16[1024,1024]{1,0:T(8,128)(2,1)S(1)}, bf16[1024,1024]{1,0:T(8,128)(2,1)}, u32[]{:S(2)}) copy-start(bf16[1024,1024]{1,0:T(8,128)(2,1)} %w_mid_ref.3) | copy-start | bytes 6291460
  13.4 5.9 %copy-start.2 = (bf16[1024,128]{1,0:T(8,128)(2,1)S(1)}, bf16[1024,128]{1,0:T(8,128)(2,1)}, u32[]{:S(2)}) copy-start(bf16[1024,128]{1,0:T(8,128)(2,1)} %w_out_ref.1) | copy-start | bytes 786436
  13.4 5.9 %copy-start.3 = (s32[3,1024]{1,0:T(4,128)S(1)}, s32[3,1024]{1,0:T(4,128)}, u32[]{:S(2)}) copy-start(s32[3,1024]{1,0:T(4,128)} %seeds_ref.1) | copy-start | bytes 36868
  19.2 2.0 %collective-permute-start = (bf16[2048,128]{1,0:T(8,128)(2,1)S(1)}, bf16[2048,128]{1,0:T(8,128)(2,1)S(1)}, u32[]{:S(2)}, u32[]{:S(2)}) collective-permute-start(bf16[2048,128]{1,0:T(8,128)(2,1)S(1)} %get-tuple-element.35.after_ref), channel_id=1, source_target_pairs={{0,16},{16,0},{1,17},{17,1},{2,18},{18,2},{3,19},{19,3},{4,20},{20... | collective-permute-start | bytes 1572872 | tf_op jit(solution)/shard_map/exchange_grads/ppermute | solution.py:287
  21.3 10.0 %collective-permute-start.2 = (bf16[512,128]{1,0:T(8,128)(2,1)S(1)}, bf16[512,128]{1,0:T(8,128)(2,1)S(1)}, u32[]{:S(2)}, u32[]{:S(2)}) collective-permute-start(bf16[512,128]{1,0:T(8,128)(2,1)S(1)} %get-tuple-element.37.after_ref), channel_id=1, source_target_pairs={{0,32},{32,64},{64,96},{96,0},{1,33},{33,65},{65,97},{97,1},{2,34}... | collective-permute-start | bytes 393224 | tf_op jit(solution)/shard_map/exchange_grads/ppermute | solution.py:305
  21.9 9.3 %collective-permute-start.1 = (bf16[512,128]{1,0:T(8,128)(2,1)S(1)}, bf16[512,128]{1,0:T(8,128)(2,1)S(1)}, u32[]{:S(2)}, u32[]{:S(2)}) collective-permute-start(bf16[512,128]{1,0:T(8,128)(2,1)S(1)} %get-tuple-element.42), channel_id=1, source_target_pairs={{0,64},{32,96},{64,0},{96,32},{1,65},{33,97},{65,1},{97,33},{2,66}... | collective-permute-start | bytes 393224 | tf_op jit(solution)/shard_map/exchange_grads/ppermute | solution.py:305
  24.0 7.6 %collective-permute-start.3 = (bf16[512,128]{1,0:T(8,128)(2,1)S(1)}, bf16[512,128]{1,0:T(8,128)(2,1)S(1)}, u32[]{:S(2)}, u32[]{:S(2)}) collective-permute-start(bf16[512,128]{1,0:T(8,128)(2,1)S(1)} %get-tuple-element.43), channel_id=1, source_target_pairs={{0,96},{32,0},{64,32},{96,64},{1,97},{33,1},{65,33},{97,65},{2,98}... | collective-permute-start | bytes 393224 | tf_op jit(solution)/shard_map/exchange_grads/ppermute | solution.py:305
  31.1 2.8 %collective-permute-start.5 = (bf16[1024,512]{1,0:T(8,128)(2,1)S(1)}, bf16[1024,512]{1,0:T(8,128)(2,1)S(1)}, u32[]{:S(2)}, u32[]{:S(2)}) collective-permute-start(bf16[1024,512]{1,0:T(8,128)(2,1)S(1)} %get-tuple-element.48), channel_id=1, source_target_pairs={{0,16},{16,0},{1,17},{17,1},{2,18},{18,2},{3,19},{19,3},{4,20},{20... | collective-permute-start | bytes 3145736 | tf_op jit(solution)/shard_map/ppermute | solution.py:318
  32.0 3.5 %collective-permute-start.6 = (bf16[1152,512]{1,0:T(8,128)(2,1)S(1)}, bf16[1152,512]{1,0:T(8,128)(2,1)S(1)}, u32[]{:S(2)}, u32[]{:S(2)}) collective-permute-start(bf16[1152,512]{1,0:T(8,128)(2,1)S(1)} %delta_two.1.delta_two_ref.delta_ref), channel_id=1, source_target_pairs={{0,16},{16,0},{1,17},{17,1},{2,18},{18,2},{3,19},{19,3},{4,20},{20... | collective-permute-start | bytes 3538952 | tf_op jit(solution)/shard_map/backward/ppermute | solution.py:339
  33.6 3.5 %collective-permute-start.4 = (bf16[1024,512]{1,0:T(8,128)(2,1)S(1)}, bf16[1024,512]{1,0:T(8,128)(2,1)S(1)}, u32[]{:S(2)}, u32[]{:S(2)}) collective-permute-start(bf16[1024,512]{1,0:T(8,128)(2,1)S(1)} %delta_one.1.delta_ref), channel_id=1, source_target_pairs={{0,16},{16,0},{1,17},{17,1},{2,18},{18,2},{3,19},{19,3},{4,20},{20... | collective-permute-start | bytes 3145736 | tf_op jit(solution)/shard_map/backward/ppermute | solution.py:349
  39.5 26.7 %all-to-all-start.1 = ((bf16[16,32,1152]{2,1,0:T(8,128)(2,1)}), bf16[16,32,1152]{2,1,0:T(8,128)(2,1)S(1)}, u32[]{:S(2)}, u32[]{:S(2)}) async-start(bf16[16,32,1152]{2,1,0:T(8,128)(2,1)} %bitcast.4), calls=%async_computation.1 | async-start | bytes 2359296 | tf_op jit(solution)/shard_map/sum_devices/all_to_all | solution.py:371
  46.6 15.0 %collective-permute-start.8 = (bf16[128,1024]{1,0:T(8,128)(2,1)S(1)}, bf16[128,1024]{1,0:T(8,128)(2,1)S(1)}, u32[]{:S(2)}, u32[]{:S(2)}) collective-permute-start(bf16[128,1024]{1,0:T(8,128)(2,1)S(1)} %get-tuple-element.49.after_ref), channel_id=1, source_target_pairs={{0,32},{32,64},{64,96},{96,0},{1,33},{33,65},{65,97},{97,1},{2,34}... | collective-permute-start | bytes 786440 | tf_op jit(solution)/shard_map/sum_devices/ppermute | solution.py:361
  47.7 13.9 %collective-permute-start.7 = (bf16[128,1024]{1,0:T(8,128)(2,1)S(1)}, bf16[128,1024]{1,0:T(8,128)(2,1)S(1)}, u32[]{:S(2)}, u32[]{:S(2)}) collective-permute-start(bf16[128,1024]{1,0:T(8,128)(2,1)S(1)} %get-tuple-element.51), channel_id=1, source_target_pairs={{0,64},{32,96},{64,0},{96,32},{1,65},{33,97},{65,1},{97,33},{2,66}... | collective-permute-start | bytes 786440 | tf_op jit(solution)/shard_map/sum_devices/ppermute | solution.py:361
  49.9 12.2 %collective-permute-start.9 = (bf16[128,1024]{1,0:T(8,128)(2,1)S(1)}, bf16[128,1024]{1,0:T(8,128)(2,1)S(1)}, u32[]{:S(2)}, u32[]{:S(2)}) collective-permute-start(bf16[128,1024]{1,0:T(8,128)(2,1)S(1)} %get-tuple-element.52), channel_id=1, source_target_pairs={{0,96},{32,0},{64,32},{96,64},{1,97},{33,1},{65,33},{97,65},{2,98}... | collective-permute-start | bytes 786440 | tf_op jit(solution)/shard_map/sum_devices/ppermute | solution.py:361
  66.2 12.2 %all-to-all-start.2 = ((bf16[16,8,1024]{2,1,0:T(8,128)(2,1)}), bf16[16,8,1024]{2,1,0:T(8,128)(2,1)S(1)}, u32[]{:S(2)}, u32[]{:S(2)}) async-start(bf16[16,8,1024]{2,1,0:T(8,128)(2,1)} %bitcast.6), calls=%async_computation.2 | async-start | bytes 524288 | tf_op jit(solution)/shard_map/sum_devices/all_to_all | solution.py:390
  70.0 8.3 %collective-permute-start.10 = (f32[8,1152]{1,0:T(8,128)S(1)}, f32[8,1152]{1,0:T(8,128)S(1)}, u32[]{:S(2)}, u32[]{:S(2)}) collective-permute-start(f32[8,1152]{1,0:T(8,128)S(1)} %get-tuple-element.54), channel_id=1, source_target_pairs={{0,64},{32,96},{64,0},{96,32},{1,65},{33,97},{65,1},{97,33},{2,66}... | collective-permute-start | bytes 110600 | tf_op jit(solution)/shard_map/sum_devices/ppermute | solution.py:389
  72.7 5.7 %collective-permute-start.11 = (f32[8,1152]{1,0:T(8,128)S(1)}, f32[8,1152]{1,0:T(8,128)S(1)}, u32[]{:S(2)}, u32[]{:S(2)}) collective-permute-start(f32[8,1152]{1,0:T(8,128)S(1)} %get-tuple-element.55), channel_id=1, source_target_pairs={{0,32},{32,64},{64,96},{96,0},{1,33},{33,65},{65,97},{97,1},{2,34}... | collective-permute-start | bytes 110600 | tf_op jit(solution)/shard_map/sum_devices/ppermute | solution.py:389
  73.6 4.7 %collective-permute-start.12 = (f32[8,1152]{1,0:T(8,128)S(1)}, f32[8,1152]{1,0:T(8,128)S(1)}, u32[]{:S(2)}, u32[]{:S(2)}) collective-permute-start(f32[8,1152]{1,0:T(8,128)S(1)} %get-tuple-element.56), channel_id=1, source_target_pairs={{0,96},{32,0},{64,32},{96,64},{1,97},{33,1},{65,33},{97,65},{2,98}... | collective-permute-start | bytes 110600 | tf_op jit(solution)/shard_map/sum_devices/ppermute | solution.py:389
